TPU v7x, 128 devices: a whole 4x4x4 slice. The times are simulated.
128 devices in a mesh: row: 8 (over x, z_lo), col: 16 (over y, z_hi, core).
Axes of the slice: x: 4, y: 4, z: 4 (z_hi: 2, z_lo: 2; z = z_hi * 2 + z_lo), core: 2. Of those that a mesh axis runs over, the one named last changes fastest.
Arguments:
- coupling: bfloat16 [3, 256, 65536], P(None, None, ('row', 'col')), may hold values from -6 to 6
- right_coupling: bfloat16 [3, 256, 16384], P(None, None, ('col', 'row')), may hold values from -0.21875 to 0.21875
- upper_inverse: bfloat16 [3, 256, 256], replicated, as said below
- lower_inverse: bfloat16 [3, 256, 256], replicated
- block_mask: int32 [3, 512], P(None, ('row', 'col')), may hold values 0 or 1
- block_map: int32 [512], replicated, may hold values from 0 to 511, as said below
Outputs:
- schur_update: bfloat16 [65536, 16384], P('row', 'col')
Inputs may be any that keep to these rules, and one draw needn't show every extreme that they name: upper_inverse[k] is upper triangular and lower_inverse[k] lower triangular, with diagonal entries from 0.5 to 1.5. `block_map`: a permutation of the 512 blocks that keeps each block within its aligned group of 64 blocks.
All inputs are finite; a program needn't handle non-finite values. No bound on the sum of `block_mask` on one device may be relied on, other than what follows from the above.
Results may differ from a plain program's by a relative error of at most 0.0058.
Values may be sent and summed in bfloat16 or wider, within the bound.
No kernel may reach another device: no remote copies, remote signals or barrier semaphores. Data moves between devices by JAX's collectives and lax.ppermute only.
A program may use at most 192 MiB of HBM per device.

v0:
```python
import jax
import jax.numpy as jnp
from jax import lax
from jax.sharding import PartitionSpec as P

BW = 128


def relay_rows(solved):
    n_panels = solved.shape[0]
    n_width = solved.shape[1]
    shard_cols = solved.shape[2]
    n_row = lax.axis_size("row")
    n_col = lax.axis_size("col")
    devices = n_row * n_col
    piece_cols = shard_cols // devices
    pieces = solved.reshape(n_panels, n_width, devices, piece_cols)
    landed = lax.all_to_all(pieces, ("row", "col"), split_axis=2, concat_axis=2, tiled=True)
    return lax.all_gather(landed.reshape(n_panels, n_width, shard_cols), "col", axis=2, tiled=True)


def reorder_blocks(row_data, block_map):
    n_panels = row_data.shape[0]
    n_width = row_data.shape[1]
    row_span = row_data.shape[2]
    groups = row_span // BW
    first_block = lax.axis_index("row") * groups
    local_map = lax.dynamic_slice_in_dim(block_map, first_block, groups) - first_block
    blocks = row_data.reshape(n_panels, n_width, groups, BW)
    return jnp.take(blocks, local_map, axis=2).reshape(n_panels, n_width, row_span)


def contract(left_part, right_part):
    left_flat = left_part.reshape(-1, left_part.shape[2])
    right_flat = right_part.reshape(-1, right_part.shape[2])
    return lax.dot_general(
        left_flat, right_flat, (((0,), (0,)), ((), ())), preferred_element_type=jnp.float32
    )


def local(coupling, right_coupling, upper_inverse, lower_inverse, block_mask, block_map):
    widened = jnp.repeat(block_mask.astype(jnp.bfloat16), BW, axis=1)
    masked = coupling * widened[:, None, :]
    solved = jnp.einsum(
        "kij,kin->kjn", upper_inverse, masked, preferred_element_type=jnp.float32
    ).astype(jnp.bfloat16)
    right_local = jnp.einsum(
        "kij,kjn->kin", lower_inverse, right_coupling, preferred_element_type=jnp.float32
    ).astype(jnp.bfloat16)
    window = lax.all_gather(right_local, "row", axis=2, tiled=True)
    row_data = reorder_blocks(relay_rows(solved), block_map)
    running = contract(row_data, window)
    return (-running).astype(jnp.bfloat16)


def solution(mesh):
    placed = (
        P(None, None, ("row", "col")),
        P(None, None, ("col", "row")),
        P(),
        P(),
        P(None, ("row", "col")),
        P(),
    )
    return jax.shard_map(
        local, mesh=mesh, in_specs=placed, out_specs=P("row", "col"), check_vma=False
    )
```

profile of v0, /device:TPU:35, one launch (start us, length us, event | category | flops | bytes accessed | tf_op | source)
XLA Modules:
  0.0 223.1 jit_solution(4686276868024854686)
XLA Ops:
  6.5 0.0 copy-start
  6.5 0.0 all-gather.3.cloned.1.call-start
  6.5 0.7 convert_element_type.15
  7.3 0.1 broadcast_bitcast_fusion
  7.4 0.2 copy-done
  7.5 1.6 fusion.2
  9.1 0.2 reshape.50
  9.3 0.3 copy.15
  9.6 24.6 %all_to_all.5 = bf16[3,256,128,4]{1,3,0,2:T(4,128)(2,1)S(1)} all-to-all(bf16[3,256,128,4]{1,3,0,2:T(4,128)(2,1)S(1)} %copy.15), channel_id=1, replica_groups=mesh['row'=8,'col'=16] {'row','col'}, dimensions={2} | all-to-all | bytes 1572864 | tf_op jit(solution)/shard_map/all_to_all | solution.py:18
  34.2 0.3 copy.16
  34.5 1.1 reshape.51
  35.6 0.0 all-gather.3.cloned.1.call-update
  35.6 0.0 all-gather.5.cloned.1.call-start
  35.6 2.0 convolution_convert_fusion.1
  37.6 0.0 all-gather.5.cloned.1.call-update
  37.6 0.8 compare_and_fusion
  38.4 85.6 %all-gather.3.cloned.1.call-done = bf16[3,256,8192]{1,2,0:T(8,128)(2,1)} async-done(((bf16[3,256,512]{1,2,0:T(8,128)(2,1)}), bf16[3,256,8192]{1,2,0:T(8,128)(2,1)}) %all-gather.3.cloned.1.call-update) | async-done | bytes 12582928 | tf_op jit(solution)/shard_map/all_gather | solution.py:19
  124.0 16.6 %copy.17 = bf16[3,256,64,128]{3,1,2,0:T(8,128)(2,1)} copy(bf16[3,256,64,128]{1,3,2,0:T(8,128)(2,1)} %bitcast.24) | data formatting | bytes 25165824 | tf_op jit(solution)/shard_map/reshape | solution.py:29
  140.6 11.9 %gather_fusion = bf16[64,3,256,128]{3,2,1,0:T(8,128)(2,1)} fusion(bf16[3,256,64,128]{3,1,2,0:T(8,128)(2,1)} %copy.17, s32[1024]{0:T(1024)S(1)} %pad_clamp_fusion), kind=kCustom, calls=%fused_computation | custom fusion | bytes 25166080 | tf_op jit(solution)/shard_map/jit(_take)/gather | solution.py:30
  152.5 6.6 %select_bitcast_fusion = bf16[3,256,64,128]{3,1,0,2:T(8,128)(2,1)S(1)} fusion(bf16[64,3,256,128]{3,2,1,0:T(8,128)(2,1)} %gather_fusion, pred[64]{0:T(512)(128)(4,1)S(1)} %get-tuple-element.5), kind=kLoop, calls=%fused_computation.4 | loop fusion | flops 6291456 | bytes 25165888 | tf_op jit(solution)/shard_map/jit(_take)/select_n | solution.py:30
  159.1 30.6 %copy.18 = bf16[3,256,64,128]{3,2,1,0:T(8,128)(2,1)} copy(bf16[3,256,64,128]{3,1,0,2:T(8,128)(2,1)S(1)} %select_bitcast_fusion) | data formatting | bytes 25165824 | tf_op jit(solution)/shard_map/jit(_take)/select_n | solution.py:30
  189.7 0.0 all-gather.5.cloned.1.call-done
  189.7 0.0 copy-start.1
  189.7 26.6 %negate_convert_fusion = bf16[8192,1024]{1,0:T(8,128)(2,1)} fusion(bf16[768,1024]{1,0:T(8,128)(2,1)} %bitcast.27, bf16[96,8,64,128]{3,2,1,0:T(8,128)(2,1)} %bitcast.25), kind=kOutput, calls=%fused_computation.1 | convolution fusion | flops 12901679104 | bytes 30932992 | tf_op jit(solution)/shard_map/dot_general | solution.py:36
  216.3 0.0 copy-done.1
  (2 shorter events, 0.0 us)
Async XLA Ops:
  6.5 1.0 copy-start
  6.5 117.5 %all-gather.3.cloned.1.call-start = ((), (), s32[]{:S(2)}) async-start(), calls=%async_computation.1 | async-start | bytes 13369344 | tf_op jit(solution)/shard_map/all_gather | solution.py:19
  35.6 154.1 %all-gather.5.cloned.1.call-start = ((), (), s32[]{:S(2)}) async-start(), calls=%async_computation.2 | async-start | bytes 1769472 | tf_op jit(solution)/shard_map/all_gather | solution.py:50
  189.7 26.6 %copy-start.1 = (bf16[3,256,256]{2,1,0:T(8,128)(2,1)S(1)}, bf16[3,256,256]{2,1,0:T(8,128)(2,1)}, u32[]{:S(2)}) copy-start(bf16[3,256,256]{2,1,0:T(8,128)(2,1)} %param.8) | copy-start | bytes 1179652
Sparse Core Ops, SparseCore 0:
  35.7 88.2 all-gather.2
  125.6 42.4 all-gather.4
where the time goes:
time: 226 us; the launch traced here: 223 us
  waiting for transfers between devices  85.6 us (38%)
  local copies, waits for them, and re-layouts  61.2 us (27%)
  matrix products  30.2 us (13%)
  blocking collectives  24.6 us (11%)
  between operations  13.4 us (6%)
  other arithmetic  8.1 us (4%)
    all_gather x1, waiting for transfers between devices, relay_rows(): lax.all_gather(landed.reshape(n_panels, n_width, shard_cols), 'col', axis...  85.6 us
    select_n x1, local copies, waits for them, and re-layouts, reorder_blocks(): jnp.take(blocks, local_map, axis=2).reshape(n_panels, n_width, row_span)  30.6 us
    dot_general x1, matrix products, contract(): lax.dot_general(left_flat, right_flat, (((0,), (0,)), ((), ())), preferre...  26.6 us
    all_to_all x1, blocking collectives, relay_rows(): lax.all_to_all(pieces, ('row', 'col'), split_axis=2, concat_axis=2, tiled...  24.6 us
    reshape x1, local copies, waits for them, and re-layouts, reorder_blocks(): blocks = row_data.reshape(n_panels, n_width, groups, BW)  16.6 us
    gather x1, local copies, waits for them, and re-layouts, reorder_blocks(): jnp.take(blocks, local_map, axis=2).reshape(n_panels, n_width, row_span)  11.9 us
    select_n x1, other arithmetic, reorder_blocks(): jnp.take(blocks, local_map, axis=2).reshape(n_panels, n_width, row_span)  6.59 us
  transfers between devices with their start and end apart: 2, of which 1 were waited for; matrix products, arithmetic and copies ran while one was open for 31% of the time, Pallas kernels for 0%

commit v1 on v0

v1 whole, which is shorter than its diff:
```python
import functools

import jax
import jax.numpy as jnp
from jax import lax
from jax.experimental import pallas as pl
from jax.experimental.pallas import tpu as pltpu
from jax.sharding import PartitionSpec as P

BF = jnp.bfloat16
F32 = jnp.float32
AXES = ("row", "col")
KF = 768
UR = 16
ANY = pl.BlockSpec(memory_space=pl.ANY)
VM = pl.BlockSpec(memory_space=pltpu.VMEM)
SM = pl.BlockSpec(memory_space=pltpu.SMEM)


def coords(d):
    row, col = divmod(d, 16)
    x, zl = divmod(row, 2)
    y, rest = divmod(col, 4)
    zh, core = divmod(rest, 2)
    return x, y, zh * 2 + zl, core


def linear(x, y, z, core):
    x, y, z = x % 4, y % 4, z % 4
    return (x * 2 + z % 2) * 16 + y * 4 + (z // 2) * 2 + core


def permute(a, to):
    return lax.ppermute(a, AXES, [(d, linear(*to(*coords(d)))) for d in range(128)])


def shift(a, dx=0, dy=0, dz=0, dc=0):
    return permute(a, lambda x, y, z, c: (x + dx, y + dy, z + dz, c ^ dc))


R4 = range(4)
XZ = [[linear(x, y, z, c) for x in R4 for z in R4] for y in R4 for c in (0, 1)]
ZZ = [[linear(x, y, z, c) for z in R4] for x in R4 for y in R4 for c in (0, 1)]


def exchange(a, groups):
    return lax.all_to_all(a, AXES, split_axis=0, concat_axis=0, tiled=True, axis_index_groups=groups)


def arr(*shape, dtype=BF):
    return jax.ShapeDtypeStruct(shape, dtype)


def cost(flops, nbytes):
    return pl.CostEstimate(flops=flops, bytes_accessed=nbytes, transcendentals=0)


def place_of(pos):
    row, col = pos[0], pos[1]
    return row // 2, col // 4, (col // 2) % 2 * 2 + row % 2, col % 2


def run(copies):
    for c in copies:
        c.start()
    for c in copies:
        c.wait()


def solve_kernel(pos, mask, coupling, upper, a0, a12, b, c_v, u_v, hold, sem):
    copies = []
    for k in range(3):
        copies.append(pltpu.make_async_copy(coupling.at[k], c_v.at[k], sem.at[k, 0]))
        copies.append(pltpu.make_async_copy(upper.at[k], u_v.at[k], sem.at[k, 1]))
    for c in copies:
        c.start()
    for k in range(3):
        copies[2 * k].wait()
        copies[2 * k + 1].wait()
        row = jnp.concatenate(
            [jnp.broadcast_to(mask[k : k + 1, j : j + 1], (1, 128)) for j in range(4)], axis=1
        )
        masked = c_v[k] * row.astype(F32).astype(BF)
        solved = lax.dot_general(
            masked, u_v[k], (((0,), (0,)), ((), ())), preferred_element_type=F32
        )
        hold[:, :, :, k * 256 : (k + 1) * 256] = solved.astype(BF).reshape(8, 4, UR, 256)
    x, _, z, _ = place_of(pos)
    for to in range(16):
        target = to // 4 * 2 + to % 2
        a0[to] = hold[target, 0]
        a12[to] = hold[target, 1:3]
    for dx in range(4):
        for e in range(2):
            b[dx, e] = hold[lax.rem(x + dx, 4) * 2 + lax.rem(z + e, 2), 3]


def solve(pos, mask, coupling, upper):
    return pl.pallas_call(
        solve_kernel,
        out_shape=(arr(16, UR, KF), arr(16, 2, UR, KF), arr(4, 2, UR, KF)),
        in_specs=[SM, VM, ANY, ANY],
        out_specs=(VM,) * 3,
        scratch_shapes=[
            pltpu.VMEM((3, 256, 512), BF),
            pltpu.VMEM((3, 256, 256), BF),
            pltpu.VMEM((8, 4, UR, KF), BF),
            pltpu.SemaphoreType.DMA((3, 2)),
        ],
        compiler_params=pltpu.CompilerParams(vmem_limit_bytes=16 << 20),
        cost_estimate=cost(2 * 512 * 256 * 768, 4 << 20),
    )(pos, mask, coupling, upper)


def after_y_kernel(pos, own, below, above, far, o0, o1, o2, o3):
    _, y, _, _ = place_of(pos)
    for dy, src in ((0, own), (3, below), (1, above), (2, far)):
        for dx, out in enumerate((o0, o1, o2, o3)):
            out[lax.rem(y + dy, 4)] = src[dx]


def after_y(pos, *parts):
    return pl.pallas_call(
        after_y_kernel,
        out_shape=(arr(4, 2, UR, KF),) * 4,
        in_specs=[SM] + [VM] * 4,
        out_specs=(VM,) * 4,
        compiler_params=pltpu.CompilerParams(vmem_limit_bytes=4 << 20),
        cost_estimate=cost(0, 2 << 20),
    )(pos, *parts)


def after_x_kernel(pos, own, below, above, far, out):
    x, _, z, _ = place_of(pos)
    for dx, src in ((0, own), (3, below), (1, above), (2, far)):
        for dz in range(4):
            for y in range(4):
                out[lax.rem(z + dz, 4), lax.rem(x + dx, 4), y] = src[y, dz % 2]


def after_x(pos, *parts):
    return pl.pallas_call(
        after_x_kernel,
        out_shape=arr(4, 4, 4, UR, KF),
        in_specs=[SM] + [VM] * 4,
        out_specs=VM,
        compiler_params=pltpu.CompilerParams(vmem_limit_bytes=4 << 20),
        cost_estimate=cost(0, 3 << 20),
    )(pos, *parts)


def move_kernel(where, *refs):
    ins, outs = refs[: -len(where)], refs[-len(where) :]
    for out, pieces in zip(outs, where):
        for to, (i, at) in enumerate(pieces):
            out[to] = ins[i][at]


def move(where, shapes, *ins):
    return pl.pallas_call(
        functools.partial(move_kernel, where),
        out_shape=tuple(arr(*s) for s in shapes),
        in_specs=[VM] * len(ins),
        out_specs=(VM,) * len(where),
        compiler_params=pltpu.CompilerParams(vmem_limit_bytes=4 << 20),
        cost_estimate=cost(0, 1 << 20),
    )(*ins)


def halves(below, above):
    where = ([(0, 0), (0, 1)], [(1, 2), (1, 3)])
    return move(where, ((2, 4, UR, KF),) * 2, below, above)


def split(both):
    where = tuple([(0, (i, g)) for i in range(16)] for g in range(2))
    first, second = move(where, ((16, UR, KF),) * 2, both)
    return first.reshape(4, 4, UR, KF), second.reshape(4, 4, UR, KF)


def stack(a, b):
    return move(([(0, ...), (1, ...)],), ((2, KF, 128),), a, b)[0]


def window_kernel(pos, own, below, above, far, lower, out, right):
    x, _, z, _ = place_of(pos)
    for dx, src in ((0, own), (3, below), (1, above), (2, far)):
        for e in range(2):
            r = lax.rem(x + dx, 4) * 2 + lax.rem(z + e, 2)
            right[:, pl.ds(pl.multiple_of(r * 128, 128), 128)] = src[e]
    for k in range(3):
        rows = slice(k * 256, (k + 1) * 256)
        solved = jnp.dot(lower[k], right[rows], preferred_element_type=F32)
        out[rows] = (-solved).astype(BF)


def window(pos, parts, lower):
    return pl.pallas_call(
        window_kernel,
        out_shape=arr(KF, 1024),
        in_specs=[SM] + [VM] * 5,
        out_specs=VM,
        scratch_shapes=[pltpu.VMEM((KF, 1024), BF)],
        compiler_params=pltpu.CompilerParams(vmem_limit_bytes=16 << 20),
        cost_estimate=cost(2 * 768 * 256 * 1024, 4 << 20),
    )(pos, *parts, lower)


def contract_kernel(group, z_major, n_mine, has_base, *refs):
    pos, place, right = refs[:3]
    parts = refs[3 : 3 + 2 * n_mine]
    out, left, stage, out_sem = refs[-4:]
    _, y0, _, core = place_of(pos)

    def fill(u):
        for whose, mine in ((core, parts[:n_mine]), (1 - core, parts[n_mine:])):
            if z_major:
                for z in range(4):
                    left[u % 2, whose, z] = mine[0][z, u]
            else:
                own, below, above, far_low, far_high = mine
                left[u % 2, whose, y0] = own[u]
                left[u % 2, whose, lax.rem(y0 + 3, 4)] = below[u]
                left[u % 2, whose, lax.rem(y0 + 1, 4)] = above[u]
                far = far_low[u] if u < 2 else far_high[u - 2]
                left[u % 2, whose, lax.rem(y0 + 2, 4)] = far

    def stores(u):
        made = []
        for p in range(4):
            at = place[(group * 4 + p) * 4 + u]
            rows = pl.ds(pl.multiple_of(at * 128, 128), 128)
            made.append(pltpu.make_async_copy(stage.at[u % 2, p], out.at[rows], out_sem.at[u % 2, p]))
        return made

    low = lax.broadcasted_iota(jnp.int32, (1, 1, 8, 256), 2) < 4
    for u in range(4):
        fill(u)
        if u >= 2:
            for c in stores(u - 2):
                c.wait()
        flat = left[u % 2].reshape(512, KF)
        for j in range(4):
            cols = slice(j * 256, (j + 1) * 256)
            acc = jnp.dot(flat, right[:, cols], preferred_element_type=F32)
            acc = acc.reshape(2, 16, 2, 8, 256)
            c0, c1 = acc[0], acc[1]
            even = jnp.where(low, c0, pltpu.roll(c1, 4, 2))
            odd = jnp.where(low, pltpu.roll(c0, 4, 2), c1)
            for half, made in enumerate((even, odd)):
                for pair in range(2):
                    for y in range(4):
                        for zl in range(2):
                            at = [
                                made[z * 4 + y if z_major else y * 4 + z, pair]
                                for z in (zl, zl + 2)
                            ]
                            r0 = (zl * 4 + y) * 16
                            stage[u % 2, pair * 2 + half, r0 : r0 + 16, cols] = (
                                jnp.concatenate(at, axis=0).astype(BF)
                            )
        for c in stores(u):
            c.start()
    for u in (2, 3):
        for c in stores(u):
            c.wait()


def contract(group, z_major, pos, place, right, mine, other, base):
    ins = [pos, place, right, *mine, *other]
    specs = [SM, SM] + [VM] * (len(ins) - 2)
    if base is not None:
        ins.append(base)
        specs.append(ANY)
    rows = 4 * 512
    return pl.pallas_call(
        functools.partial(contract_kernel, group, z_major, len(mine), base is not None),
        out_shape=arr(8192, 1024),
        in_specs=specs,
        out_specs=ANY,
        scratch_shapes=[
            pltpu.VMEM((2, 2, 4, 4, UR, KF), BF),
            pltpu.VMEM((2, 4, 128, 1024), BF),
            pltpu.SemaphoreType.DMA((2, 4)),
        ],
        input_output_aliases={} if base is None else {len(ins) - 1: 0},
        compiler_params=pltpu.CompilerParams(vmem_limit_bytes=14 << 20),
        cost_estimate=cost(2 * rows * KF * 1024, rows * (KF + 1024) * 2),
    )(*ins)


def after(value, *done):
    return lax.optimization_barrier((value, *done))[0]


def forward(own, below, above):
    low, high = halves(below, above)
    return [own, below, above, shift(low, dy=1), shift(high, dy=-1)]


def local(coupling, right_coupling, upper_inverse, lower_inverse, block_mask, block_map):
    row, col = lax.axis_index("row"), lax.axis_index("col")
    pos = jnp.stack([row, col]).astype(jnp.int32)

    here = lax.dynamic_slice_in_dim(block_map, row * 64, 64) - row * 64
    slots = jnp.arange(64, dtype=jnp.int32)
    place = jnp.sum(
        jnp.where(here[None, :] == slots[:, None], slots[None, :], 0), axis=1, dtype=jnp.int32
    )

    coupling, place = lax.optimization_barrier((coupling, place))

    a0, a12, b = solve(pos, block_mask, coupling, upper_inverse)
    raw = right_coupling.reshape(KF, 128)
    b_below, b_above, b_far = shift(b, dy=1), shift(b, dy=-1), shift(b, dy=2)
    w_other = permute(raw, lambda x, y, z, c: (x, y, z ^ 1, c))
    s0 = exchange(a0, XZ).reshape(4, 4, UR, KF)

    a12 = after(a12, b_below, b_above, b_far, w_other, s0)
    s12 = exchange(a12, XZ)
    g0, g1, g2, g3 = after_y(pos, b, b_below, b_above, b_far)
    x_below, x_above, x_far = shift(g1, dx=1), shift(g3, dx=-1), shift(g2, dx=2)
    below0, above0 = shift(s0, dy=1), shift(s0, dy=-1)

    bz = after_x(pos, g0, x_below, x_above, x_far)
    s12, bz, below0, above0 = lax.optimization_barrier((s12, bz, below0, above0))
    mine3 = [exchange(bz, ZZ)]
    s1, s2 = split(s12)
    mine0 = forward(s0, below0, above0)

    pair = after(stack(raw, w_other), x_below, x_above, x_far)
    w_below, w_above = shift(pair, dx=1), shift(pair, dx=-1)
    w_far = shift(after(pair, w_below, w_above), dx=2)
    right = window(pos, [pair, w_below, w_above, w_far], lower_inverse)

    s1 = after(s1, below0, above0)
    below1, above1 = shift(s1, dy=1), shift(s1, dy=-1)
    mine1 = forward(s1, below1, above1)
    s2 = after(s2, below1, above1)
    below2, above2 = shift(s2, dy=1), shift(s2, dy=-1)
    mine2 = forward(s2, below2, above2)

    def swapped(mine):
        return [shift(m, dc=1) for m in mine]

    out = contract(0, False, pos, place, right, mine0, swapped(mine0), None)
    out = contract(1, False, pos, place, right, mine1, swapped(mine1), out)
    out = contract(3, True, pos, place, right, mine3, swapped(mine3), out)
    return contract(2, False, pos, place, right, mine2, swapped(mine2), out)


def solution(mesh):
    placed = (
        P(None, None, ("row", "col")),
        P(None, None, ("col", "row")),
        P(),
        P(),
        P(None, ("row", "col")),
        P(),
    )
    return jax.shard_map(
        local, mesh=mesh, in_specs=placed, out_specs=P("row", "col"), check_vma=False
    )
```

time: 226 us -> 151 us (0.67)
  starting transfers between devices: 0.04 us -> 70.4 us
  waiting for transfers between devices: 85.6 us -> 28.1 us
  local copies, waits for them, and re-layouts: 61.2 us -> 16.8 us
  Pallas kernels: 0 us -> 32.9 us
  matrix products: 30.2 us -> 0 us
  blocking collectives: 24.6 us -> 0 us
  between operations: 13.4 us -> 0.43 us
  other arithmetic: 8.1 us -> 0.94 us
    all_gather x2 -> x0, waiting for transfers between devices: 85.6 us -> none  [the longest x1 85.6 us: relay_rows(): lax.all_gather(landed.reshape(n_panels, n_width, shard_cols), 'col', axis...]
    ppermute x0 -> x38, starting transfers between devices: none -> 52.2 us  [permute(): lax.ppermute(a, AXES, [(d, linear(*to(*coords(d)))) for d in range(128)])]
    pallas_call x0 -> x13, Pallas kernels: none -> 32.9 us  [the longest x4 23.8 us: contract(): pl.pallas_call(functools.partial(contract_kernel, group, z_major, len(min...]
    select_n x1 -> x0, local copies, waits for them, and re-layouts: 30.6 us -> none  [reorder_blocks(): jnp.take(blocks, local_map, axis=2).reshape(n_panels, n_width, row_span)]
    dot_general x3 -> x0, matrix products: 30.2 us -> none  [the longest x1 26.6 us: contract(): lax.dot_general(left_flat, right_flat, (((0,), (0,)), ((), ())), preferre...]
    ppermute x0 -> x38, waiting for transfers between devices: none -> 28.1 us  [permute(): lax.ppermute(a, AXES, [(d, linear(*to(*coords(d)))) for d in range(128)])]
    all_to_all x1 -> x0, blocking collectives: 24.6 us -> none  [relay_rows(): lax.all_to_all(pieces, ('row', 'col'), split_axis=2, concat_axis=2, tiled...]
    all_to_all x0 -> x3, starting transfers between devices: none -> 18.2 us  [exchange(): lax.all_to_all(a, AXES, split_axis=0, concat_axis=0, tiled=True, axis_ind...]
  transfers between devices with their start and end apart: 2 -> 41, of which waited for: 1 -> 8; matrix products, arithmetic and copies ran while one was open for 31% -> 0% of each run, Pallas kernels for 0% -> 16%
where the time goes in v1:
time: 151 us; the launch traced here: 150 us
  starting transfers between devices  70.4 us (47%)
  Pallas kernels  32.9 us (22%)
  waiting for transfers between devices  28.1 us (19%)
  local copies, waits for them, and re-layouts  16.8 us (11%)
    ppermute x38, starting transfers between devices, permute(): lax.ppermute(a, AXES, [(d, linear(*to(*coords(d)))) for d in range(128)])  52.2 us
    ppermute x38, waiting for transfers between devices, permute(): lax.ppermute(a, AXES, [(d, linear(*to(*coords(d)))) for d in range(128)])  28.1 us
    pallas_call x4, Pallas kernels, contract(): pl.pallas_call(functools.partial(contract_kernel, group, z_major, len(min...  23.8 us
    all_to_all x3, starting transfers between devices, exchange(): lax.all_to_all(a, AXES, split_axis=0, concat_axis=0, tiled=True, axis_ind...  18.2 us
    unnamed x40, local copies, waits for them, and re-layouts  16.8 us
    pallas_call x1, Pallas kernels, solve(): pl.pallas_call(solve_kernel, out_shape=(arr(16, UR, KF), arr(16, 2, UR, K...  3.36 us
  transfers between devices with their start and end apart: 41, of which 8 were waited for; matrix products, arithmetic and copies ran while one was open for 0% of the time, Pallas kernels for 16%

profile of v1, /device:TPU:35, one launch (start us, length us, event | category | flops | bytes accessed | tf_op | source)
XLA Modules:
  0.0 149.7 jit_solution(2967077536907790975)
XLA Ops:
  3.8 3.4 %shard_map.65 = (bf16[16,16,768]{2,1,0:T(8,128)(2,1)}, bf16[16,2,16,768]{3,2,1,0:T(8,128)(2,1)}, bf16[4,2,16,768]{3,2,1,0:T(8,128)(2,1)S(1)}) custom-call(s32[2]{0:T(128)S(1)} %pad_add_fusion.pos.refs_0_, s32[3,4]{1,0:T(4,128)S(1)} %copy-done.19, bf16[3,256,512]{2,1,0:T(8,128)(2,1)S(1)} %copy-done.3, bf16[3,256,256]{2,1,0:T(8,128)(2,1)S(1)} %copy-done.6), custom_call_target="tpu_custom_call" | custom-call | flops 201326592 | bytes 4194304 | tf_op jit(solution)/shard_map/pallas_call | solution.py:99
  7.1 7.3 %all-to-all-start = ((bf16[16,16,768]{2,1,0:T(8,128)(2,1)}), bf16[16,16,768]{2,1,0:T(8,128)(2,1)S(1)}, u32[]{:S(2)}, u32[]{:S(2)}) async-start(bf16[16,16,768]{2,1,0:T(8,128)(2,1)} %get-tuple-element.40), calls=%async_computation | async-start | bytes 786432 | tf_op jit(solution)/shard_map/all_to_all | solution.py:47
  14.5 1.3 collective-permute-start.1
  15.8 1.5 %collective-permute-start.2 = (bf16[4,2,16,768]{3,2,1,0:T(8,128)(2,1)S(1)}, bf16[4,2,16,768]{3,2,1,0:T(8,128)(2,1)S(1)}, u32[]{:S(2)}, u32[]{:S(2)}) collective-permute-start(bf16[4,2,16,768]{3,2,1,0:T(8,128)(2,1)S(1)} %get-tuple-element.33.own), channel_id=1, source_target_pairs={{0,12},{1,13},{2,14},{3,15},{4,0},{5,1},{6,2},{7,3},{8,4},{9,5},{1... | collective-permute-start | bytes 589832 | tf_op jit(solution)/shard_map/ppermute | solution.py:34
  17.3 1.6 %collective-permute-start.3 = (bf16[4,2,16,768]{3,2,1,0:T(8,128)(2,1)S(1)}, bf16[4,2,16,768]{3,2,1,0:T(8,128)(2,1)S(1)}, u32[]{:S(2)}, u32[]{:S(2)}) collective-permute-start(bf16[4,2,16,768]{3,2,1,0:T(8,128)(2,1)S(1)} %get-tuple-element.33.own), channel_id=1, source_target_pairs={{0,8},{1,9},{2,10},{3,11},{4,12},{5,13},{6,14},{7,15},{8,0},{9,1},... | collective-permute-start | bytes 589832 | tf_op jit(solution)/shard_map/ppermute | solution.py:34
  19.1 1.8 %collective-permute-done.1.below = bf16[4,2,16,768]{3,2,1,0:T(8,128)(2,1)S(1)} collective-permute-done((bf16[4,2,16,768]{3,2,1,0:T(8,128)(2,1)S(1)}, bf16[4,2,16,768]{3,2,1,0:T(8,128)(2,1)S(1)}, u32[]{:S(2)}, u32[]{:S(2)}) %collective-permute-start.1) | collective-permute-done | bytes 196640 | tf_op jit(solution)/shard_map/ppermute | solution.py:34
  20.9 5.3 %collective-permute-done.3.far = bf16[4,2,16,768]{3,2,1,0:T(8,128)(2,1)S(1)} collective-permute-done((bf16[4,2,16,768]{3,2,1,0:T(8,128)(2,1)S(1)}, bf16[4,2,16,768]{3,2,1,0:T(8,128)(2,1)S(1)}, u32[]{:S(2)}, u32[]{:S(2)}) %collective-permute-start.3) | collective-permute-done | bytes 196640 | tf_op jit(solution)/shard_map/ppermute | solution.py:34
  27.0 6.7 %all-to-all-start.1 = ((bf16[16,2,16,768]{3,2,1,0:T(8,128)(2,1)}), bf16[16,2,16,768]{3,2,1,0:T(8,128)(2,1)S(1)}, u32[]{:S(2)}, u32[]{:S(2)}) async-start(bf16[16,2,16,768]{3,2,1,0:T(8,128)(2,1)} %get-tuple-element.41), calls=%async_computation.1 | async-start | bytes 1572864 | tf_op jit(solution)/shard_map/all_to_all | solution.py:47
  34.2 2.1 %collective-permute-start.11 = (bf16[4,4,16,768]{3,2,1,0:T(8,128)(2,1)S(1)}, bf16[4,4,16,768]{3,2,1,0:T(8,128)(2,1)S(1)}, u32[]{:S(2)}, u32[]{:S(2)}) collective-permute-start(bf16[4,4,16,768]{3,2,1,0:T(8,128)(2,1)S(1)} %bitcast.7), channel_id=1, source_target_pairs={{0,12},{1,13},{2,14},{3,15},{4,0},{5,1},{6,2},{7,3},{8,4},{9,5},{1... | collective-permute-start | bytes 1179656 | tf_op jit(solution)/shard_map/ppermute | solution.py:34
  36.9 1.3 collective-permute-start.4
  38.4 1.8 %collective-permute-start.6 = (bf16[4,2,16,768]{3,2,1,0:T(8,128)(2,1)S(1)}, bf16[4,2,16,768]{3,2,1,0:T(8,128)(2,1)S(1)}, u32[]{:S(2)}, u32[]{:S(2)}) collective-permute-start(bf16[4,2,16,768]{3,2,1,0:T(8,128)(2,1)S(1)} %get-tuple-element.36), channel_id=1, source_target_pairs={{0,64},{1,65},{2,66},{3,67},{4,68},{5,69},{6,70},{7,71},{8,72},{9,... | collective-permute-start | bytes 589832 | tf_op jit(solution)/shard_map/ppermute | solution.py:34
  40.2 6.4 %collective-permute-done.4.below = bf16[4,2,16,768]{3,2,1,0:T(8,128)(2,1)S(1)} collective-permute-done((bf16[4,2,16,768]{3,2,1,0:T(8,128)(2,1)S(1)}, bf16[4,2,16,768]{3,2,1,0:T(8,128)(2,1)S(1)}, u32[]{:S(2)}, u32[]{:S(2)}) %collective-permute-start.4) | collective-permute-done | bytes 196640 | tf_op jit(solution)/shard_map/ppermute | solution.py:34
  47.4 3.2 %collective-permute-done.6.far = bf16[4,2,16,768]{3,2,1,0:T(8,128)(2,1)S(1)} collective-permute-done((bf16[4,2,16,768]{3,2,1,0:T(8,128)(2,1)S(1)}, bf16[4,2,16,768]{3,2,1,0:T(8,128)(2,1)S(1)}, u32[]{:S(2)}, u32[]{:S(2)}) %collective-permute-start.6) | collective-permute-done | bytes 196640 | tf_op jit(solution)/shard_map/ppermute | solution.py:34
  50.6 1.8 %shard_map.68 = bf16[4,4,4,16,768]{4,3,2,1,0:T(8,128)(2,1)} custom-call(s32[2]{0:T(128)S(1)} %pad_add_fusion.pos.refs_0_, bf16[4,2,16,768]{3,2,1,0:T(8,128)(2,1)S(1)} %get-tuple-element.42.own, bf16[4,2,16,768]{3,2,1,0:T(8,128)(2,1)S(1)} %collective-permute-done.4.below, bf16[4,2,16,768]{3,2,1,0:T(8,128)(2,1)S(1)} %collective-permute-done.5.above, ...), custom_call_target="tpu_custom_call" | custom-call | bytes 3145728 | tf_op jit(solution)/shard_map/pallas_call | solution.py:142
  53.2 4.2 %all-to-all-start.2 = ((bf16[4,4,4,16,768]{4,3,2,1,0:T(8,128)(2,1)}), bf16[4,4,4,16,768]{4,3,2,1,0:T(8,128)(2,1)S(1)}, u32[]{:S(2)}, u32[]{:S(2)}) async-start(bf16[4,4,4,16,768]{4,3,2,1,0:T(8,128)(2,1)} %shard_map.68), calls=%async_computation.2 | async-start | bytes 3145728 | tf_op jit(solution)/shard_map/all_to_all | solution.py:47
  59.4 1.5 collective-permute-start.8
  60.8 4.7 %collective-permute-start.33 = (bf16[4,4,16,768]{3,2,1,0:T(8,128)(2,1)S(1)}, bf16[4,4,16,768]{3,2,1,0:T(8,128)(2,1)S(1)}, u32[]{:S(2)}, u32[]{:S(2)}) collective-permute-start(bf16[4,4,16,768]{3,2,1,0:T(8,128)(2,1)S(1)} %bitcast.8), channel_id=1, source_target_pairs={{0,1},{1,0},{2,3},{3,2},{4,5},{5,4},{6,7},{7,6},{8,9},{9,8},{10,11... | collective-permute-start | bytes 1179656 | tf_op jit(solution)/shard_map/ppermute | solution.py:34
  67.8 3.1 %collective-permute-start.9 = (bf16[2,768,128]{2,1,0:T(8,128)(2,1)S(1)}, bf16[2,768,128]{2,1,0:T(8,128)(2,1)S(1)}, u32[]{:S(2)}, u32[]{:S(2)}) collective-permute-start(bf16[2,768,128]{2,1,0:T(8,128)(2,1)S(1)} %shard_map.64.own), channel_id=1, source_target_pairs={{0,64},{1,65},{2,66},{3,67},{4,68},{5,69},{6,70},{7,71},{8,72},{9,... | collective-permute-start | bytes 1179656 | tf_op jit(solution)/shard_map/ppermute | solution.py:34
  72.8 2.3 %collective-permute-start.13 = (bf16[4,4,16,768]{3,2,1,0:T(8,128)(2,1)}, bf16[4,4,16,768]{3,2,1,0:T(8,128)(2,1)S(1)}, u32[]{:S(2)}, u32[]{:S(2)}) collective-permute-start(bf16[4,4,16,768]{3,2,1,0:T(8,128)(2,1)} %bitcast.5.refs_3_), channel_id=1, source_target_pairs={{0,12},{1,13},{2,14},{3,15},{4,0},{5,1},{6,2},{7,3},{8,4},{9,5},{1... | collective-permute-start | bytes 1179656 | tf_op jit(solution)/shard_map/ppermute | solution.py:34
  77.7 2.7 %collective-permute-start.32 = (bf16[2,4,16,768]{3,2,1,0:T(8,128)(2,1)}, bf16[2,4,16,768]{3,2,1,0:T(8,128)(2,1)}, u32[]{:S(2)}, u32[]{:S(2)}) collective-permute-start(bf16[2,4,16,768]{3,2,1,0:T(8,128)(2,1)} %get-tuple-element.56), channel_id=1, source_target_pairs={{0,12},{1,13},{2,14},{3,15},{4,0},{5,1},{6,2},{7,3},{8,4},{9,5},{1... | collective-permute-start | bytes 589832 | tf_op jit(solution)/shard_map/ppermute | solution.py:34
  81.1 11.2 %collective-permute-start.23 = (bf16[4,4,4,16,768]{4,3,2,1,0:T(8,128)(2,1)S(1)}, bf16[4,4,4,16,768]{4,3,2,1,0:T(8,128)(2,1)S(1)}, u32[]{:S(2)}, u32[]{:S(2)}) collective-permute-start(bf16[4,4,4,16,768]{4,3,2,1,0:T(8,128)(2,1)S(1)} %all-to-all-done.2.refs_3_), channel_id=1, source_target_pairs={{0,1},{1,0},{2,3},{3,2},{4,5},{5,4},{6,7},{7,6},{8,9},{9,8},{10,11... | collective-permute-start | bytes 4718600 | tf_op jit(solution)/shard_map/ppermute | solution.py:34
  92.3 2.4 %collective-permute-start.34 = (bf16[4,4,16,768]{3,2,1,0:T(8,128)(2,1)S(1)}, bf16[4,4,16,768]{3,2,1,0:T(8,128)(2,1)S(1)}, u32[]{:S(2)}, u32[]{:S(2)}) collective-permute-start(bf16[4,4,16,768]{3,2,1,0:T(8,128)(2,1)S(1)} %collective-permute-done.10.refs_0_.refs_4_), channel_id=1, source_target_pairs={{0,1},{1,0},{2,3},{3,2},{4,5},{5,4},{6,7},{7,6},{8,9},{9,8},{10,11... | collective-permute-start | bytes 1179656 | tf_op jit(solution)/shard_map/ppermute | solution.py:34
  97.0 3.2 %collective-permute-start.15 = (bf16[4,4,16,768]{3,2,1,0:T(8,128)(2,1)}, bf16[4,4,16,768]{3,2,1,0:T(8,128)(2,1)S(1)}, u32[]{:S(2)}, u32[]{:S(2)}) collective-permute-start(bf16[4,4,16,768]{3,2,1,0:T(8,128)(2,1)} %bitcast.11), channel_id=1, source_target_pairs={{0,12},{1,13},{2,14},{3,15},{4,0},{5,1},{6,2},{7,3},{8,4},{9,5},{1... | collective-permute-start | bytes 1179656 | tf_op jit(solution)/shard_map/ppermute | solution.py:34
  100.8 8.8 %collective-permute-done.14.refs_0_.refs_4_ = bf16[4,4,16,768]{3,2,1,0:T(8,128)(2,1)S(1)} collective-permute-done((bf16[4,4,16,768]{3,2,1,0:T(8,128)(2,1)}, bf16[4,4,16,768]{3,2,1,0:T(8,128)(2,1)S(1)}, u32[]{:S(2)}, u32[]{:S(2)}) %collective-permute-start.14) | collective-permute-done | bytes 393248 | tf_op jit(solution)/shard_map/ppermute | solution.py:34
  109.6 1.1 collective-permute-start.25
  110.8 2.1 %collective-permute-start.28 = (bf16[4,4,16,768]{3,2,1,0:T(8,128)(2,1)S(1)}, bf16[4,4,16,768]{3,2,1,0:T(8,128)(2,1)S(1)}, u32[]{:S(2)}, u32[]{:S(2)}) collective-permute-start(bf16[4,4,16,768]{3,2,1,0:T(8,128)(2,1)S(1)} %collective-permute-done.13.refs_1_.refs_5_), channel_id=1, source_target_pairs={{0,1},{1,0},{2,3},{3,2},{4,5},{5,4},{6,7},{7,6},{8,9},{9,8},{10,11... | collective-permute-start | bytes 1179656 | tf_op jit(solution)/shard_map/ppermute | solution.py:34
  116.8 1.6 %shard_map.67.refs_2_ = bf16[768,1024]{1,0:T(8,128)(2,1)S(1)} custom-call(s32[2]{0:T(128)S(1)} %pad_add_fusion.pos.refs_0_, bf16[2,768,128]{2,1,0:T(8,128)(2,1)S(1)} %shard_map.64.own, bf16[2,768,128]{2,1,0:T(8,128)(2,1)S(1)} %copy-done.9, bf16[2,768,128]{2,1,0:T(8,128)(2,1)S(1)} %copy-done.11, bf16[2,768,128]{2,1,0:T(8,128)(2,1)S(1)} %copy-done.13, ...), custom_call_target="tpu_custom_call" | custom-call | flops 402653184 | bytes 4194304 | tf_op jit(solution)/shard_map/pallas_call | solution.py:198
  121.1 6.2 %shard_map.73.refs_13_ = bf16[8192,1024]{1,0:T(8,128)(2,1)} custom-call(s32[2]{0:T(128)S(1)} %pad_add_fusion.pos.refs_0_, s32[64]{0:T(128)S(1)} %select_reduce_fusion.refs_1_, bf16[768,1024]{1,0:T(8,128)(2,1)S(1)} %shard_map.67.refs_2_, bf16[4,4,16,768]{3,2,1,0:T(8,128)(2,1)S(1)} %bitcast.9, ...), custom_call_target="tpu_custom_call" | custom-call | flops 3221225472 | bytes 7340032 | tf_op jit(solution)/shard_map/pallas_call | solution.py:276
  127.5 2.9 %collective-permute-start.17 = (bf16[2,4,16,768]{3,2,1,0:T(8,128)(2,1)S(1)}, bf16[2,4,16,768]{3,2,1,0:T(8,128)(2,1)S(1)}, u32[]{:S(2)}, u32[]{:S(2)}) collective-permute-start(bf16[2,4,16,768]{3,2,1,0:T(8,128)(2,1)S(1)} %get-tuple-element.51), channel_id=1, source_target_pairs={{0,12},{1,13},{2,14},{3,15},{4,0},{5,1},{6,2},{7,3},{8,4},{9,5},{1... | collective-permute-start | bytes 589832 | tf_op jit(solution)/shard_map/ppermute | solution.py:34
  131.0 6.2 %shard_map.74.refs_5_ = bf16[8192,1024]{1,0:T(8,128)(2,1)} custom-call(s32[2]{0:T(128)S(1)} %pad_add_fusion.pos.refs_0_, s32[64]{0:T(128)S(1)} %select_reduce_fusion.refs_1_, bf16[768,1024]{1,0:T(8,128)(2,1)S(1)} %shard_map.67.refs_2_, bf16[4,4,16,768]{3,2,1,0:T(8,128)(2,1)} %bitcast.5.refs_3_, ...), custom_call_target="tpu_custom_call", output_to_operand_aliasing={{}: (13, {})} | custom-call | flops 3221225472 | bytes 7340032 | tf_op jit(solution)/shard_map/pallas_call | solution.py:276
  138.0 5.8 %shard_map.75.refs_13_ = bf16[8192,1024]{1,0:T(8,128)(2,1)} custom-call(s32[2]{0:T(128)S(1)} %pad_add_fusion.pos.refs_0_, s32[64]{0:T(128)S(1)} %select_reduce_fusion.refs_1_, bf16[768,1024]{1,0:T(8,128)(2,1)S(1)} %shard_map.67.refs_2_, bf16[4,4,4,16,768]{4,3,2,1,0:T(8,128)(2,1)S(1)} %all-to-all-done.2.refs_3_, ...), custom_call_target="tpu_custom_call", output_to_operand_aliasing={{}: (5, {})} | custom-call | flops 3221225472 | bytes 7340032 | tf_op jit(solution)/shard_map/pallas_call | solution.py:276
  143.8 5.7 %shard_map.76 = bf16[8192,1024]{1,0:T(8,128)(2,1)} custom-call(s32[2]{0:T(128)S(1)} %pad_add_fusion.pos.refs_0_, s32[64]{0:T(128)S(1)} %select_reduce_fusion.refs_1_, bf16[768,1024]{1,0:T(8,128)(2,1)S(1)} %shard_map.67.refs_2_, bf16[4,4,16,768]{3,2,1,0:T(8,128)(2,1)S(1)} %bitcast.13, ...), custom_call_target="tpu_custom_call", output_to_operand_aliasing={{}: (13, {})} | custom-call | flops 3221225472 | bytes 7340032 | tf_op jit(solution)/shard_map/pallas_call | solution.py:276
  (106 shorter events, 28.0 us)
Async XLA Ops:
  7.1 19.2 %all-to-all-start = ((bf16[16,16,768]{2,1,0:T(8,128)(2,1)}), bf16[16,16,768]{2,1,0:T(8,128)(2,1)S(1)}, u32[]{:S(2)}, u32[]{:S(2)}) async-start(bf16[16,16,768]{2,1,0:T(8,128)(2,1)} %get-tuple-element.40), calls=%async_computation | async-start | bytes 786432 | tf_op jit(solution)/shard_map/all_to_all | solution.py:47
  17.3 9.0 %collective-permute-start.3 = (bf16[4,2,16,768]{3,2,1,0:T(8,128)(2,1)S(1)}, bf16[4,2,16,768]{3,2,1,0:T(8,128)(2,1)S(1)}, u32[]{:S(2)}, u32[]{:S(2)}) collective-permute-start(bf16[4,2,16,768]{3,2,1,0:T(8,128)(2,1)S(1)} %get-tuple-element.33.own), channel_id=1, source_target_pairs={{0,8},{1,9},{2,10},{3,11},{4,12},{5,13},{6,14},{7,15},{8,0},{9,1},... | collective-permute-start | bytes 589832 | tf_op jit(solution)/shard_map/ppermute | solution.py:34
  18.8 7.4 %collective-permute-start = (bf16[768,128]{1,0:T(8,128)(2,1)}, bf16[768,128]{1,0:T(8,128)(2,1)S(1)}, u32[]{:S(2)}, u32[]{:S(2)}) collective-permute-start(bf16[768,128]{1,0:T(8,128)(2,1)} %bitcast.14), channel_id=1, source_target_pairs={{0,16},{1,17},{2,18},{3,19},{4,20},{5,21},{6,22},{7,23},{8,24},{9,... | collective-permute-start | bytes 589832 | tf_op jit(solution)/shard_map/ppermute | solution.py:34
  27.0 26.2 %all-to-all-start.1 = ((bf16[16,2,16,768]{3,2,1,0:T(8,128)(2,1)}), bf16[16,2,16,768]{3,2,1,0:T(8,128)(2,1)S(1)}, u32[]{:S(2)}, u32[]{:S(2)}) async-start(bf16[16,2,16,768]{3,2,1,0:T(8,128)(2,1)} %get-tuple-element.41), calls=%async_computation.1 | async-start | bytes 1572864 | tf_op jit(solution)/shard_map/all_to_all | solution.py:47
  33.6 18.8 %collective-permute-start.10 = (bf16[4,4,16,768]{3,2,1,0:T(8,128)(2,1)S(1)}, bf16[4,4,16,768]{3,2,1,0:T(8,128)(2,1)S(1)}, u32[]{:S(2)}, u32[]{:S(2)}) collective-permute-start(bf16[4,4,16,768]{3,2,1,0:T(8,128)(2,1)S(1)} %bitcast.6), channel_id=1, source_target_pairs={{0,4},{1,5},{2,6},{3,7},{4,8},{5,9},{6,10},{7,11},{8,12},{9,13},{1... | collective-permute-start | bytes 1179656 | tf_op jit(solution)/shard_map/ppermute | solution.py:34
  34.2 18.2 %collective-permute-start.11 = (bf16[4,4,16,768]{3,2,1,0:T(8,128)(2,1)S(1)}, bf16[4,4,16,768]{3,2,1,0:T(8,128)(2,1)S(1)}, u32[]{:S(2)}, u32[]{:S(2)}) collective-permute-start(bf16[4,4,16,768]{3,2,1,0:T(8,128)(2,1)S(1)} %bitcast.7), channel_id=1, source_target_pairs={{0,12},{1,13},{2,14},{3,15},{4,0},{5,1},{6,2},{7,3},{8,4},{9,5},{1... | collective-permute-start | bytes 1179656 | tf_op jit(solution)/shard_map/ppermute | solution.py:34
  36.9 9.8 %collective-permute-start.4 = (bf16[4,2,16,768]{3,2,1,0:T(8,128)(2,1)S(1)}, bf16[4,2,16,768]{3,2,1,0:T(8,128)(2,1)S(1)}, u32[]{:S(2)}, u32[]{:S(2)}) collective-permute-start(bf16[4,2,16,768]{3,2,1,0:T(8,128)(2,1)S(1)} %get-tuple-element.34), channel_id=1, source_target_pairs={{0,32},{1,33},{2,34},{3,35},{4,36},{5,37},{6,38},{7,39},{8,40},{9,... | collective-permute-start | bytes 589832 | tf_op jit(solution)/shard_map/ppermute | solution.py:34
  38.2 9.2 %collective-permute-start.5 = (bf16[4,2,16,768]{3,2,1,0:T(8,128)(2,1)S(1)}, bf16[4,2,16,768]{3,2,1,0:T(8,128)(2,1)S(1)}, u32[]{:S(2)}, u32[]{:S(2)}) collective-permute-start(bf16[4,2,16,768]{3,2,1,0:T(8,128)(2,1)S(1)} %get-tuple-element.35), channel_id=1, source_target_pairs={{0,96},{1,97},{2,98},{3,99},{4,100},{5,101},{6,102},{7,103},{8,104... | collective-permute-start | bytes 589832 | tf_op jit(solution)/shard_map/ppermute | solution.py:34
  38.4 12.1 %collective-permute-start.6 = (bf16[4,2,16,768]{3,2,1,0:T(8,128)(2,1)S(1)}, bf16[4,2,16,768]{3,2,1,0:T(8,128)(2,1)S(1)}, u32[]{:S(2)}, u32[]{:S(2)}) collective-permute-start(bf16[4,2,16,768]{3,2,1,0:T(8,128)(2,1)S(1)} %get-tuple-element.36), channel_id=1, source_target_pairs={{0,64},{1,65},{2,66},{3,67},{4,68},{5,69},{6,70},{7,71},{8,72},{9,... | collective-permute-start | bytes 589832 | tf_op jit(solution)/shard_map/ppermute | solution.py:34
  53.2 27.9 %all-to-all-start.2 = ((bf16[4,4,4,16,768]{4,3,2,1,0:T(8,128)(2,1)}), bf16[4,4,4,16,768]{4,3,2,1,0:T(8,128)(2,1)S(1)}, u32[]{:S(2)}, u32[]{:S(2)}) async-start(bf16[4,4,4,16,768]{4,3,2,1,0:T(8,128)(2,1)} %shard_map.68), calls=%async_computation.2 | async-start | bytes 3145728 | tf_op jit(solution)/shard_map/all_to_all | solution.py:47
  59.3 7.0 %collective-permute-start.7 = (bf16[2,768,128]{2,1,0:T(8,128)(2,1)S(1)}, bf16[2,768,128]{2,1,0:T(8,128)(2,1)S(1)}, u32[]{:S(2)}, u32[]{:S(2)}) collective-permute-start(bf16[2,768,128]{2,1,0:T(8,128)(2,1)S(1)} %shard_map.64.own), channel_id=1, source_target_pairs={{0,32},{1,33},{2,34},{3,35},{4,36},{5,37},{6,38},{7,39},{8,40},{9,... | collective-permute-start | bytes 1179656 | tf_op jit(solution)/shard_map/ppermute | solution.py:34
  59.4 7.7 %collective-permute-start.8 = (bf16[2,768,128]{2,1,0:T(8,128)(2,1)S(1)}, bf16[2,768,128]{2,1,0:T(8,128)(2,1)S(1)}, u32[]{:S(2)}, u32[]{:S(2)}) collective-permute-start(bf16[2,768,128]{2,1,0:T(8,128)(2,1)S(1)} %shard_map.64.own), channel_id=1, source_target_pairs={{0,96},{1,97},{2,98},{3,99},{4,100},{5,101},{6,102},{7,103},{8,104... | collective-permute-start | bytes 1179656 | tf_op jit(solution)/shard_map/ppermute | solution.py:34
  60.8 16.1 %collective-permute-start.33 = (bf16[4,4,16,768]{3,2,1,0:T(8,128)(2,1)S(1)}, bf16[4,4,16,768]{3,2,1,0:T(8,128)(2,1)S(1)}, u32[]{:S(2)}, u32[]{:S(2)}) collective-permute-start(bf16[4,4,16,768]{3,2,1,0:T(8,128)(2,1)S(1)} %bitcast.8), channel_id=1, source_target_pairs={{0,1},{1,0},{2,3},{3,2},{4,5},{5,4},{6,7},{7,6},{8,9},{9,8},{10,11... | collective-permute-start | bytes 1179656 | tf_op jit(solution)/shard_map/ppermute | solution.py:34
  67.8 12.5 %collective-permute-start.9 = (bf16[2,768,128]{2,1,0:T(8,128)(2,1)S(1)}, bf16[2,768,128]{2,1,0:T(8,128)(2,1)S(1)}, u32[]{:S(2)}, u32[]{:S(2)}) collective-permute-start(bf16[2,768,128]{2,1,0:T(8,128)(2,1)S(1)} %shard_map.64.own), channel_id=1, source_target_pairs={{0,64},{1,65},{2,66},{3,67},{4,68},{5,69},{6,70},{7,71},{8,72},{9,... | collective-permute-start | bytes 1179656 | tf_op jit(solution)/shard_map/ppermute | solution.py:34
  72.4 22.6 %collective-permute-start.12 = (bf16[4,4,16,768]{3,2,1,0:T(8,128)(2,1)}, bf16[4,4,16,768]{3,2,1,0:T(8,128)(2,1)S(1)}, u32[]{:S(2)}, u32[]{:S(2)}) collective-permute-start(bf16[4,4,16,768]{3,2,1,0:T(8,128)(2,1)} %bitcast.5.refs_3_), channel_id=1, source_target_pairs={{0,4},{1,5},{2,6},{3,7},{4,8},{5,9},{6,10},{7,11},{8,12},{9,13},{1... | collective-permute-start | bytes 1179656 | tf_op jit(solution)/shard_map/ppermute | solution.py:34
  72.8 22.5 %collective-permute-start.13 = (bf16[4,4,16,768]{3,2,1,0:T(8,128)(2,1)}, bf16[4,4,16,768]{3,2,1,0:T(8,128)(2,1)S(1)}, u32[]{:S(2)}, u32[]{:S(2)}) collective-permute-start(bf16[4,4,16,768]{3,2,1,0:T(8,128)(2,1)} %bitcast.5.refs_3_), channel_id=1, source_target_pairs={{0,12},{1,13},{2,14},{3,15},{4,0},{5,1},{6,2},{7,3},{8,4},{9,5},{1... | collective-permute-start | bytes 1179656 | tf_op jit(solution)/shard_map/ppermute | solution.py:34
  76.9 15.4 %collective-permute-start.31 = (bf16[2,4,16,768]{3,2,1,0:T(8,128)(2,1)}, bf16[2,4,16,768]{3,2,1,0:T(8,128)(2,1)}, u32[]{:S(2)}, u32[]{:S(2)}) collective-permute-start(bf16[2,4,16,768]{3,2,1,0:T(8,128)(2,1)} %get-tuple-element.55), channel_id=1, source_target_pairs={{0,4},{1,5},{2,6},{3,7},{4,8},{5,9},{6,10},{7,11},{8,12},{9,13},{1... | collective-permute-start | bytes 589832 | tf_op jit(solution)/shard_map/ppermute | solution.py:34
  77.7 17.1 %collective-permute-start.32 = (bf16[2,4,16,768]{3,2,1,0:T(8,128)(2,1)}, bf16[2,4,16,768]{3,2,1,0:T(8,128)(2,1)}, u32[]{:S(2)}, u32[]{:S(2)}) collective-permute-start(bf16[2,4,16,768]{3,2,1,0:T(8,128)(2,1)} %get-tuple-element.56), channel_id=1, source_target_pairs={{0,12},{1,13},{2,14},{3,15},{4,0},{5,1},{6,2},{7,3},{8,4},{9,5},{1... | collective-permute-start | bytes 589832 | tf_op jit(solution)/shard_map/ppermute | solution.py:34
  81.1 56.5 %collective-permute-start.23 = (bf16[4,4,4,16,768]{4,3,2,1,0:T(8,128)(2,1)S(1)}, bf16[4,4,4,16,768]{4,3,2,1,0:T(8,128)(2,1)S(1)}, u32[]{:S(2)}, u32[]{:S(2)}) collective-permute-start(bf16[4,4,4,16,768]{4,3,2,1,0:T(8,128)(2,1)S(1)} %all-to-all-done.2.refs_3_), channel_id=1, source_target_pairs={{0,1},{1,0},{2,3},{3,2},{4,5},{5,4},{6,7},{7,6},{8,9},{9,8},{10,11... | collective-permute-start | bytes 4718600 | tf_op jit(solution)/shard_map/ppermute | solution.py:34
  97.0 12.7 %collective-permute-start.14 = (bf16[4,4,16,768]{3,2,1,0:T(8,128)(2,1)}, bf16[4,4,16,768]{3,2,1,0:T(8,128)(2,1)S(1)}, u32[]{:S(2)}, u32[]{:S(2)}) collective-permute-start(bf16[4,4,16,768]{3,2,1,0:T(8,128)(2,1)} %bitcast.10), channel_id=1, source_target_pairs={{0,4},{1,5},{2,6},{3,7},{4,8},{5,9},{6,10},{7,11},{8,12},{9,13},{1... | collective-permute-start | bytes 1179656 | tf_op jit(solution)/shard_map/ppermute | solution.py:34
  97.0 13.8 %collective-permute-start.15 = (bf16[4,4,16,768]{3,2,1,0:T(8,128)(2,1)}, bf16[4,4,16,768]{3,2,1,0:T(8,128)(2,1)S(1)}, u32[]{:S(2)}, u32[]{:S(2)}) collective-permute-start(bf16[4,4,16,768]{3,2,1,0:T(8,128)(2,1)} %bitcast.11), channel_id=1, source_target_pairs={{0,12},{1,13},{2,14},{3,15},{4,0},{5,1},{6,2},{7,3},{8,4},{9,5},{1... | collective-permute-start | bytes 1179656 | tf_op jit(solution)/shard_map/ppermute | solution.py:34
  100.2 18.9 %collective-permute-start.27 = (bf16[4,4,16,768]{3,2,1,0:T(8,128)(2,1)S(1)}, bf16[4,4,16,768]{3,2,1,0:T(8,128)(2,1)S(1)}, u32[]{:S(2)}, u32[]{:S(2)}) collective-permute-start(bf16[4,4,16,768]{3,2,1,0:T(8,128)(2,1)S(1)} %collective-permute-done.12.refs_0_.refs_4_), channel_id=1, source_target_pairs={{0,1},{1,0},{2,3},{3,2},{4,5},{5,4},{6,7},{7,6},{8,9},{9,8},{10,11... | collective-permute-start | bytes 1179656 | tf_op jit(solution)/shard_map/ppermute | solution.py:34
  100.7 17.8 %collective-permute-start.24 = (bf16[2,4,16,768]{3,2,1,0:T(8,128)(2,1)S(1)}, bf16[2,4,16,768]{3,2,1,0:T(8,128)(2,1)S(1)}, u32[]{:S(2)}, u32[]{:S(2)}) collective-permute-start(bf16[2,4,16,768]{3,2,1,0:T(8,128)(2,1)S(1)} %get-tuple-element.53), channel_id=1, source_target_pairs={{0,4},{1,5},{2,6},{3,7},{4,8},{5,9},{6,10},{7,11},{8,12},{9,13},{1... | collective-permute-start | bytes 589832 | tf_op jit(solution)/shard_map/ppermute | solution.py:34
  109.6 9.0 %collective-permute-start.25 = (bf16[2,4,16,768]{3,2,1,0:T(8,128)(2,1)S(1)}, bf16[2,4,16,768]{3,2,1,0:T(8,128)(2,1)S(1)}, u32[]{:S(2)}, u32[]{:S(2)}) collective-permute-start(bf16[2,4,16,768]{3,2,1,0:T(8,128)(2,1)S(1)} %get-tuple-element.54), channel_id=1, source_target_pairs={{0,12},{1,13},{2,14},{3,15},{4,0},{5,1},{6,2},{7,3},{8,4},{9,5},{1... | collective-permute-start | bytes 589832 | tf_op jit(solution)/shard_map/ppermute | solution.py:34
  110.8 16.5 %collective-permute-start.28 = (bf16[4,4,16,768]{3,2,1,0:T(8,128)(2,1)S(1)}, bf16[4,4,16,768]{3,2,1,0:T(8,128)(2,1)S(1)}, u32[]{:S(2)}, u32[]{:S(2)}) collective-permute-start(bf16[4,4,16,768]{3,2,1,0:T(8,128)(2,1)S(1)} %collective-permute-done.13.refs_1_.refs_5_), channel_id=1, source_target_pairs={{0,1},{1,0},{2,3},{3,2},{4,5},{5,4},{6,7},{7,6},{8,9},{9,8},{10,11... | collective-permute-start | bytes 1179656 | tf_op jit(solution)/shard_map/ppermute | solution.py:34
  118.5 9.0 %collective-permute-start.29 = (bf16[2,4,16,768]{3,2,1,0:T(8,128)(2,1)S(1)}, bf16[2,4,16,768]{3,2,1,0:T(8,128)(2,1)S(1)}, u32[]{:S(2)}, u32[]{:S(2)}) collective-permute-start(bf16[2,4,16,768]{3,2,1,0:T(8,128)(2,1)S(1)} %collective-permute-done.24.refs_6_), channel_id=1, source_target_pairs={{0,1},{1,0},{2,3},{3,2},{4,5},{5,4},{6,7},{7,6},{8,9},{9,8},{10,11... | collective-permute-start | bytes 589832 | tf_op jit(solution)/shard_map/ppermute | solution.py:34
  118.6 11.8 %collective-permute-start.30 = (bf16[2,4,16,768]{3,2,1,0:T(8,128)(2,1)S(1)}, bf16[2,4,16,768]{3,2,1,0:T(8,128)(2,1)S(1)}, u32[]{:S(2)}, u32[]{:S(2)}) collective-permute-start(bf16[2,4,16,768]{3,2,1,0:T(8,128)(2,1)S(1)} %collective-permute-done.25.refs_7_), channel_id=1, source_target_pairs={{0,1},{1,0},{2,3},{3,2},{4,5},{5,4},{6,7},{7,6},{8,9},{9,8},{10,11... | collective-permute-start | bytes 589832 | tf_op jit(solution)/shard_map/ppermute | solution.py:34
  119.1 11.8 %collective-permute-start.16 = (bf16[2,4,16,768]{3,2,1,0:T(8,128)(2,1)S(1)}, bf16[2,4,16,768]{3,2,1,0:T(8,128)(2,1)S(1)}, u32[]{:S(2)}, u32[]{:S(2)}) collective-permute-start(bf16[2,4,16,768]{3,2,1,0:T(8,128)(2,1)S(1)} %get-tuple-element.50), channel_id=1, source_target_pairs={{0,4},{1,5},{2,6},{3,7},{4,8},{5,9},{6,10},{7,11},{8,12},{9,13},{1... | collective-permute-start | bytes 589832 | tf_op jit(solution)/shard_map/ppermute | solution.py:34
  127.3 16.4 %collective-permute-start.18 = (bf16[4,4,16,768]{3,2,1,0:T(8,128)(2,1)S(1)}, bf16[4,4,16,768]{3,2,1,0:T(8,128)(2,1)S(1)}, u32[]{:S(2)}, u32[]{:S(2)}) collective-permute-start(bf16[4,4,16,768]{3,2,1,0:T(8,128)(2,1)S(1)} %bitcast.12), channel_id=1, source_target_pairs={{0,1},{1,0},{2,3},{3,2},{4,5},{5,4},{6,7},{7,6},{8,9},{9,8},{10,11... | collective-permute-start | bytes 1179656 | tf_op jit(solution)/shard_map/ppermute | solution.py:34
  127.5 9.6 %collective-permute-start.17 = (bf16[2,4,16,768]{3,2,1,0:T(8,128)(2,1)S(1)}, bf16[2,4,16,768]{3,2,1,0:T(8,128)(2,1)S(1)}, u32[]{:S(2)}, u32[]{:S(2)}) collective-permute-start(bf16[2,4,16,768]{3,2,1,0:T(8,128)(2,1)S(1)} %get-tuple-element.51), channel_id=1, source_target_pairs={{0,12},{1,13},{2,14},{3,15},{4,0},{5,1},{6,2},{7,3},{8,4},{9,5},{1... | collective-permute-start | bytes 589832 | tf_op jit(solution)/shard_map/ppermute | solution.py:34
  130.4 13.3 %collective-permute-start.19 = (bf16[4,4,16,768]{3,2,1,0:T(8,128)(2,1)S(1)}, bf16[4,4,16,768]{3,2,1,0:T(8,128)(2,1)S(1)}, u32[]{:S(2)}, u32[]{:S(2)}) collective-permute-start(bf16[4,4,16,768]{3,2,1,0:T(8,128)(2,1)S(1)} %collective-permute-done.14.refs_0_.refs_4_), channel_id=1, source_target_pairs={{0,1},{1,0},{2,3},{3,2},{4,5},{5,4},{6,7},{7,6},{8,9},{9,8},{10,11... | collective-permute-start | bytes 1179656 | tf_op jit(solution)/shard_map/ppermute | solution.py:34
  130.9 12.9 %collective-permute-start.20 = (bf16[4,4,16,768]{3,2,1,0:T(8,128)(2,1)S(1)}, bf16[4,4,16,768]{3,2,1,0:T(8,128)(2,1)S(1)}, u32[]{:S(2)}, u32[]{:S(2)}) collective-permute-start(bf16[4,4,16,768]{3,2,1,0:T(8,128)(2,1)S(1)} %collective-permute-done.15.refs_1_.refs_5_), channel_id=1, source_target_pairs={{0,1},{1,0},{2,3},{3,2},{4,5},{5,4},{6,7},{7,6},{8,9},{9,8},{10,11... | collective-permute-start | bytes 1179656 | tf_op jit(solution)/shard_map/ppermute | solution.py:34
  (29 other events, 105.0 us)

commit v2 on v1

v2 whole, which is shorter than its diff:
```python
import functools

import jax
import jax.numpy as jnp
from jax import lax
from jax.experimental import pallas as pl
from jax.experimental.pallas import tpu as pltpu
from jax.sharding import PartitionSpec as P

BF = jnp.bfloat16
F32 = jnp.float32
AXES = ("row", "col")
KF = 768
DEPTH = 3
UR = 16
ANY = pl.BlockSpec(memory_space=pl.ANY)
VM = pl.BlockSpec(memory_space=pltpu.VMEM)
SM = pl.BlockSpec(memory_space=pltpu.SMEM)


def coords(d):
    row, col = divmod(d, 16)
    x, zl = divmod(row, 2)
    y, rest = divmod(col, 4)
    zh, core = divmod(rest, 2)
    return x, y, zh * 2 + zl, core


def linear(x, y, z, core):
    x, y, z = x % 4, y % 4, z % 4
    return (x * 2 + z % 2) * 16 + y * 4 + (z // 2) * 2 + core


def permute(a, to):
    return lax.ppermute(a, AXES, [(d, linear(*to(*coords(d)))) for d in range(128)])


def shift(a, dx=0, dy=0, dz=0, dc=0):
    return permute(a, lambda x, y, z, c: (x + dx, y + dy, z + dz, c ^ dc))


R4 = range(4)
XZ = [[linear(x, y, z, c) for x in R4 for z in R4] for y in R4 for c in (0, 1)]
XX = [[linear(x, y, z, c) for x in R4] for y in R4 for z in R4 for c in (0, 1)]
YC = [[y * 4 + zh * 2 + c for y in R4 for c in (0, 1)] for zh in (0, 1)]
ZZ = [[linear(x, y, z, c) for z in R4] for x in R4 for y in R4 for c in (0, 1)]


def exchange(a, groups):
    return lax.all_to_all(a, AXES, split_axis=0, concat_axis=0, tiled=True, axis_index_groups=groups)


def arr(*shape, dtype=BF):
    return jax.ShapeDtypeStruct(shape, dtype)


def cost(flops, nbytes):
    return pl.CostEstimate(flops=flops, bytes_accessed=nbytes, transcendentals=0)


def place_of(pos):
    row, col = pos[0], pos[1]
    return row // 2, col // 4, (col // 2) % 2 * 2 + row % 2, col % 2


def run(copies):
    for c in copies:
        c.start()
    for c in copies:
        c.wait()


def solve_kernel(pos, mask, coupling, upper, a, b, c_v, u_v, hold, sem):
    copies = []
    for k in range(3):
        copies.append(pltpu.make_async_copy(coupling.at[k], c_v.at[k], sem.at[k, 0]))
        copies.append(pltpu.make_async_copy(upper.at[k], u_v.at[k], sem.at[k, 1]))
    for c in copies:
        c.start()
    for k in range(3):
        copies[2 * k].wait()
        copies[2 * k + 1].wait()
        row = jnp.concatenate(
            [jnp.broadcast_to(mask[k : k + 1, j : j + 1], (1, 128)) for j in range(4)], axis=1
        )
        masked = c_v[k] * row.astype(F32).astype(BF)
        solved = lax.dot_general(
            masked, u_v[k], (((0,), (0,)), ((), ())), preferred_element_type=F32
        )
        hold[:, :, :, k * 256 : (k + 1) * 256] = solved.astype(BF).reshape(8, 4, UR, 256)
    x, _, z, _ = place_of(pos)
    for to in range(16):
        target = to // 4 * 2 + to % 2
        a[to] = hold[target, 0:3]
    for dx in range(4):
        for e in range(2):
            b[dx, e] = hold[lax.rem(x + dx, 4) * 2 + lax.rem(z + e, 2), 3]


def solve(pos, mask, coupling, upper):
    return pl.pallas_call(
        solve_kernel,
        out_shape=(arr(16, 3, UR, KF), arr(4, 2, UR, KF)),
        in_specs=[SM, VM, ANY, ANY],
        out_specs=(VM,) * 2,
        scratch_shapes=[
            pltpu.VMEM((3, 256, 512), BF),
            pltpu.VMEM((3, 256, 256), BF),
            pltpu.VMEM((8, 4, UR, KF), BF),
            pltpu.SemaphoreType.DMA((3, 2)),
        ],
        compiler_params=pltpu.CompilerParams(vmem_limit_bytes=60 << 20),
        cost_estimate=cost(2 * 512 * 256 * 768, 4 << 20),
    )(pos, mask, coupling, upper)


def after_y_kernel(pos, own, below, above, far, out):
    x, y, _, _ = place_of(pos)
    for dy, src in ((0, own), (3, below), (1, above), (2, far)):
        for dx in range(4):
            out[lax.rem(x + dx, 4), lax.rem(y + dy, 4)] = src[dx]


def after_y(pos, *parts):
    return pl.pallas_call(
        after_y_kernel,
        out_shape=arr(4, 4, 2, UR, KF),
        in_specs=[SM] + [VM] * 4,
        out_specs=VM,
        compiler_params=pltpu.CompilerParams(vmem_limit_bytes=4 << 20),
        cost_estimate=cost(0, 2 << 20),
    )(pos, *parts)


def after_x_kernel(pos, got, out):
    _, _, z, _ = place_of(pos)
    for x in range(4):
        for dz in range(4):
            for y in range(4):
                out[lax.rem(z + dz, 4), x, y] = got[x, y, dz % 2]


def after_x(pos, got):
    return pl.pallas_call(
        after_x_kernel,
        out_shape=arr(4, 4, 4, UR, KF),
        in_specs=[SM, VM],
        out_specs=VM,
        compiler_params=pltpu.CompilerParams(vmem_limit_bytes=4 << 20),
        cost_estimate=cost(0, 3 << 20),
    )(pos, got)


def move_kernel(where, *refs):
    ins, outs = refs[: -len(where)], refs[-len(where) :]
    for out, pieces in zip(outs, where):
        for to, (i, at) in enumerate(pieces):
            out[to] = ins[i][at]


def move(where, shapes, *ins):
    return pl.pallas_call(
        functools.partial(move_kernel, where),
        out_shape=tuple(arr(*s) for s in shapes),
        in_specs=[VM] * len(ins),
        out_specs=(VM,) * len(where),
        compiler_params=pltpu.CompilerParams(vmem_limit_bytes=4 << 20),
        cost_estimate=cost(0, 1 << 20),
    )(*ins)


def stack(a, b):
    return move(([(0, ...), (1, ...)],), ((2, KF, 128),), a, b)[0]


def window_kernel(pos, own, below, above, far, lower, out, right):
    x, _, z, _ = place_of(pos)
    for dx, src in ((0, own), (3, below), (1, above), (2, far)):
        for e in range(2):
            r = lax.rem(x + dx, 4) * 2 + lax.rem(z + e, 2)
            right[:, pl.ds(pl.multiple_of(r * 128, 128), 128)] = src[e]
    for k in range(3):
        rows = slice(k * 256, (k + 1) * 256)
        solved = jnp.dot(lower[k], right[rows], preferred_element_type=F32)
        out[rows] = (-solved).astype(BF)


def window(pos, parts, lower):
    return pl.pallas_call(
        window_kernel,
        out_shape=arr(KF, 1024),
        in_specs=[SM] + [VM] * 5,
        out_specs=VM,
        scratch_shapes=[pltpu.VMEM((KF, 1024), BF)],
        compiler_params=pltpu.CompilerParams(vmem_limit_bytes=16 << 20),
        cost_estimate=cost(2 * 768 * 256 * 1024, 4 << 20),
    )(pos, *parts, lower)


def contract_kernel(groups, gathered, *refs):
    pos, place, right = refs[:3]
    out, right_v, left, stage, r_sem, in_sem, out_sem = refs[-7:]
    _, _, _, core = place_of(pos)
    right_in = pltpu.make_async_copy(right, right_v, r_sem)
    units = [(u, i) for u in range(4) for i in range(len(groups))]

    def loads(n):
        u, i = units[n]
        if gathered:
            pairs = [(refs[3].at[:, u, :, i], left.at[n])]
        else:
            pairs = [
                (refs[3].at[:, u], left.at[n, pl.ds(core * 4, 4)]),
                (refs[4].at[:, u], left.at[n, pl.ds((1 - core) * 4, 4)]),
            ]
        return [
            pltpu.make_async_copy(src, dst, in_sem.at[n, k]) for k, (src, dst) in enumerate(pairs)
        ]

    def stores(n):
        u, i = units[n]
        made = []
        for p in range(4):
            at = place[(groups[i] * 4 + p) * 4 + u]
            rows = pl.ds(pl.multiple_of(at * 128, 128), 128)
            made.append(pltpu.make_async_copy(stage.at[n % 2, p], out.at[rows], out_sem.at[n % 2, p]))
        return made

    for c in loads(0):
        c.start()
    right_in.start()
    for n in range(1, DEPTH):
        for c in loads(n):
            c.start()
    right_in.wait()
    low = lax.broadcasted_iota(jnp.int32, (1, 1, 8, 256), 2) < 4
    for n in range(len(units)):
        for c in loads(n):
            c.wait()
        if n + DEPTH < len(units):
            for c in loads(n + DEPTH):
                c.start()
        if n >= 2:
            for c in stores(n - 2):
                c.wait()
        flat = left[n].reshape(512, KF)
        for j in range(4):
            cols = slice(j * 256, (j + 1) * 256)
            acc = jnp.dot(flat, right_v[:, cols], preferred_element_type=F32)
            if gathered:
                acc = acc.reshape(4, 2, 4, 2, 8, 256)
                c0, c1 = acc[:, 0].reshape(16, 2, 8, 256), acc[:, 1].reshape(16, 2, 8, 256)
            else:
                acc = acc.reshape(2, 16, 2, 8, 256)
                c0, c1 = acc[0], acc[1]
            even = jnp.where(low, c0, pltpu.roll(c1, 4, 2))
            odd = jnp.where(low, pltpu.roll(c0, 4, 2), c1)
            for half, made in enumerate((even, odd)):
                for pair in range(2):
                    for y in range(4):
                        for zl in range(2):
                            at = [
                                made[y * 4 + z if gathered else z * 4 + y, pair]
                                for z in (zl, zl + 2)
                            ]
                            r0 = (zl * 4 + y) * 16
                            stage[n % 2, pair * 2 + half, r0 : r0 + 16, cols] = (
                                jnp.concatenate(at, axis=0).astype(BF)
                            )
        for c in stores(n):
            c.start()
    for n in range(len(units) - 2, len(units)):
        for c in stores(n):
            c.wait()


def contract(groups, gathered, pos, place, right, parts, base):
    ins = [pos, place, right, *parts]
    if base is not None:
        ins.append(base)
    units = 4 * len(groups)
    return pl.pallas_call(
        functools.partial(contract_kernel, groups, gathered),
        out_shape=arr(8192, 1024),
        in_specs=[SM, SM] + [ANY] * (len(ins) - 2),
        out_specs=ANY,
        scratch_shapes=[
            pltpu.VMEM((KF, 1024), BF),
            pltpu.VMEM((units, 8, 4, UR, KF), BF),
            pltpu.VMEM((2, 4, 128, 1024), BF),
            pltpu.SemaphoreType.DMA,
            pltpu.SemaphoreType.DMA((units, 2)),
            pltpu.SemaphoreType.DMA((2, 4)),
        ],
        input_output_aliases={} if base is None else {len(ins) - 1: 0},
        compiler_params=pltpu.CompilerParams(vmem_limit_bytes=56 << 20),
        cost_estimate=cost(2 * units * 512 * KF * 1024, units * 512 * (KF + 1024) * 2),
    )(*ins)


def after(value, *done):
    return lax.optimization_barrier((value, *done))[0]


def local(coupling, right_coupling, upper_inverse, lower_inverse, block_mask, block_map):
    row, col = lax.axis_index("row"), lax.axis_index("col")
    pos = jnp.stack([row, col]).astype(jnp.int32)

    here = lax.dynamic_slice_in_dim(block_map, row * 64, 64) - row * 64
    slots = jnp.arange(64, dtype=jnp.int32)
    place = jnp.sum(
        jnp.where(here[None, :] == slots[:, None], slots[None, :], 0), axis=1, dtype=jnp.int32
    )

    a, b = solve(pos, block_mask, coupling, upper_inverse)
    b_below, b_above, b_far = shift(b, dy=1), shift(b, dy=-1), shift(b, dy=2)
    own, b_below, b_above, b_far = lax.optimization_barrier(
        (exchange(a, XZ).reshape(4, 4, 3, UR, KF), b_below, b_above, b_far)
    )

    whole = lax.all_gather(own, "col", axis=0, tiled=False, axis_index_groups=YC)
    raw = after(right_coupling.reshape(KF, 128), own)
    w_other = permute(raw, lambda x, y, z, c: (x, y, z ^ 1, c))
    by = after_y(pos, b, b_below, b_above, b_far)
    bx, w_other = lax.optimization_barrier((exchange(by, XX), w_other))
    pair = stack(raw, w_other)
    bz, pair = lax.optimization_barrier((after_x(pos, bx), pair))
    zs = exchange(bz, ZZ)
    w_below, w_above, w_far = shift(pair, dx=1), shift(pair, dx=-1), shift(pair, dx=2)
    zs, w_below, w_above, w_far = lax.optimization_barrier((zs, w_below, w_above, w_far))
    right = window(pos, [pair, w_below, w_above, w_far], lower_inverse)
    out = contract((3,), False, pos, place, right, [zs, shift(zs, dc=1)], None)
    return contract((0, 1, 2), True, pos, place, right, [whole], out)


def solution(mesh):
    placed = (
        P(None, None, ("row", "col")),
        P(None, None, ("col", "row")),
        P(),
        P(),
        P(None, ("row", "col")),
        P(),
    )
    return jax.shard_map(
        local, mesh=mesh, in_specs=placed, out_specs=P("row", "col"), check_vma=False
    )
```

time: 151 us -> 116 us (0.77)
  starting transfers between devices: 70.4 us -> 28 us
  local copies, waits for them, and re-layouts: 16.8 us -> 2.18 us
  between operations: 0.43 us -> 13.5 us
  waiting for transfers between devices: 28.1 us -> 36.4 us
    ppermute x38 -> x8, starting transfers between devices: 52.2 us -> 9.8 us  [permute(): lax.ppermute(a, AXES, [(d, linear(*to(*coords(d)))) for d in range(128)])]
    unnamed x40 -> x14, local copies, waits for them, and re-layouts: 16.8 us -> 2.18 us
    all_to_all x3, waiting for transfers between devices: 0.01 us -> 5.05 us  [exchange(): lax.all_to_all(a, AXES, split_axis=0, concat_axis=0, tiled=True, axis_ind...]
    all_gather x0 -> x1, waiting for transfers between devices: none -> 3.24 us  [local(): lax.all_gather(own, 'col', axis=0, tiled=False, axis_index_groups=YC)]
    pallas_call x5 -> x1, Pallas kernels: 1.66 us -> 0.03 us  [move(): pl.pallas_call(functools.partial(move_kernel, where), out_shape=tuple((ar...]
    pallas_call x6 -> x4, Pallas kernels: 27.8 us -> 28.5 us  [the longest x2 23 us: contract(): pl.pallas_call(functools.partial(contract_kernel, groups, gathered), out_...]
    ppermute x38 -> x8, waiting for transfers between devices: 28.1 us -> 28.1 us  [permute(): lax.ppermute(a, AXES, [(d, linear(*to(*coords(d)))) for d in range(128)])]
  transfers between devices with their start and end apart: 41 -> 12, of which waited for: 8 -> 9; matrix products, arithmetic and copies ran while one was open for 0% -> 1% of each run, Pallas kernels for 16% -> 11%
where the time goes in v2:
time: 116 us; the launch traced here: 114 us
  waiting for transfers between devices  36.4 us (31%)
  Pallas kernels  32 us (28%)
  starting transfers between devices  28 us (24%)
  between operations  13.5 us (12%)
  local copies, waits for them, and re-layouts  2.18 us (2%)
  other arithmetic  2.03 us (2%)
    ppermute x8, waiting for transfers between devices, permute(): lax.ppermute(a, AXES, [(d, linear(*to(*coords(d)))) for d in range(128)])  28.1 us
    pallas_call x2, Pallas kernels, contract(): pl.pallas_call(functools.partial(contract_kernel, groups, gathered), out_...  23 us
    all_to_all x3, starting transfers between devices, exchange(): lax.all_to_all(a, AXES, split_axis=0, concat_axis=0, tiled=True, axis_ind...  18.1 us
    ppermute x8, starting transfers between devices, permute(): lax.ppermute(a, AXES, [(d, linear(*to(*coords(d)))) for d in range(128)])  9.8 us
    all_to_all x3, waiting for transfers between devices, exchange(): lax.all_to_all(a, AXES, split_axis=0, concat_axis=0, tiled=True, axis_ind...  5.05 us
    pallas_call x1, Pallas kernels, solve(): pl.pallas_call(solve_kernel, out_shape=(arr(16, 3, UR, KF), arr(4, 2, UR,...  3.98 us
    all_gather x1, waiting for transfers between devices, local(): lax.all_gather(own, 'col', axis=0, tiled=False, axis_index_groups=YC)  3.24 us
  transfers between devices with their start and end apart: 12, of which 9 were waited for; matrix products, arithmetic and copies ran while one was open for 1% of the time, Pallas kernels for 11%

profile of v2, /device:TPU:35, one launch (start us, length us, event | category | flops | bytes accessed | tf_op | source)
XLA Modules:
  0.0 114.1 jit_solution(4842643983920807758)
XLA Ops:
  6.5 0.6 pad_add_fusion.pos.refs_0_
  7.2 4.0 %shard_map.64 = (bf16[16,3,16,768]{3,2,1,0:T(8,128)(2,1)}, bf16[4,2,16,768]{3,2,1,0:T(8,128)(2,1)}) custom-call(s32[2]{0:T(128)} %pad_add_fusion.pos.refs_0_, s32[3,4]{1,0:T(4,128)} %mask.1, bf16[3,256,512]{2,1,0:T(8,128)(2,1)} %coupling.1, bf16[3,256,256]{2,1,0:T(8,128)(2,1)} %upper.1), custom_call_target="tpu_custom_call" | custom-call | flops 201326592 | bytes 4194304 | tf_op jit(solution)/shard_map/pallas_call | solution.py:101
  11.2 7.5 %all-to-all-start = ((bf16[16,3,16,768]{3,2,1,0:T(8,128)(2,1)}), bf16[16,3,16,768]{3,2,1,0:T(8,128)(2,1)S(1)}, u32[]{:S(2)}, u32[]{:S(2)}) async-start(bf16[16,3,16,768]{3,2,1,0:T(8,128)(2,1)} %get-tuple-element.21), calls=%async_computation | async-start | bytes 2359296 | tf_op jit(solution)/shard_map/all_to_all | solution.py:50
  18.6 0.0 all-gather.3.cloned.1.call-start
  18.7 3.0 %collective-permute-start.2 = (bf16[4,2,16,768]{3,2,1,0:T(8,128)(2,1)S(1)}, bf16[4,2,16,768]{3,2,1,0:T(8,128)(2,1)S(1)}, u32[]{:S(2)}, u32[]{:S(2)}) collective-permute-start(bf16[4,2,16,768]{3,2,1,0:T(8,128)(2,1)S(1)} %copy-done.3), channel_id=1, source_target_pairs={{0,8},{1,9},{2,10},{3,11},{4,12},{5,13},{6,14},{7,15},{8,0},{9,1},... | collective-permute-start | bytes 589832 | tf_op jit(solution)/shard_map/ppermute | solution.py:35
  21.7 0.8 collective-permute-start.1
  22.4 0.7 collective-permute-start
  23.1 2.3 %collective-permute-done.2.far = bf16[4,2,16,768]{3,2,1,0:T(8,128)(2,1)S(1)} collective-permute-done((bf16[4,2,16,768]{3,2,1,0:T(8,128)(2,1)S(1)}, bf16[4,2,16,768]{3,2,1,0:T(8,128)(2,1)S(1)}, u32[]{:S(2)}, u32[]{:S(2)}) %collective-permute-start.2) | collective-permute-done | bytes 196640 | tf_op jit(solution)/shard_map/ppermute | solution.py:35
  25.4 5.2 %collective-permute-done.1.above = bf16[4,2,16,768]{3,2,1,0:T(8,128)(2,1)S(1)} collective-permute-done((bf16[4,2,16,768]{3,2,1,0:T(8,128)(2,1)S(1)}, bf16[4,2,16,768]{3,2,1,0:T(8,128)(2,1)S(1)}, u32[]{:S(2)}, u32[]{:S(2)}) %collective-permute-start.1) | collective-permute-done | bytes 196640 | tf_op jit(solution)/shard_map/ppermute | solution.py:35
  30.6 0.1 collective-permute-done.below
  30.7 2.1 %all-to-all-done = bf16[16,3,16,768]{3,2,1,0:T(8,128)(2,1)S(1)} async-done(((bf16[16,3,16,768]{3,2,1,0:T(8,128)(2,1)}), bf16[16,3,16,768]{3,2,1,0:T(8,128)(2,1)S(1)}, u32[]{:S(2)}, u32[]{:S(2)}) %all-to-all-start) | async-done | bytes 1179680 | tf_op jit(solution)/shard_map/all_to_all | solution.py:50
  32.8 1.0 copy-done.6
  33.9 1.5 %shard_map.65 = bf16[4,4,2,16,768]{4,3,2,1,0:T(8,128)(2,1)} custom-call(s32[2]{0:T(128)S(1)} %copy-done.4, bf16[4,2,16,768]{3,2,1,0:T(8,128)(2,1)S(1)} %copy-done.3, bf16[4,2,16,768]{3,2,1,0:T(8,128)(2,1)S(1)} %collective-permute-done.below, bf16[4,2,16,768]{3,2,1,0:T(8,128)(2,1)S(1)} %collective-permute-done.1.above, ...), custom_call_target="tpu_custom_call" | custom-call | bytes 2097152 | tf_op jit(solution)/shard_map/pallas_call | solution.py:125
  35.4 5.3 %all-to-all-start.1 = ((bf16[4,4,2,16,768]{4,3,2,1,0:T(8,128)(2,1)}), bf16[4,4,2,16,768]{4,3,2,1,0:T(8,128)(2,1)S(1)}, u32[]{:S(2)}, u32[]{:S(2)}) async-start(bf16[4,4,2,16,768]{4,3,2,1,0:T(8,128)(2,1)} %shard_map.65), calls=%async_computation.1 | async-start | bytes 1572864 | tf_op jit(solution)/shard_map/all_to_all | solution.py:50
  40.7 1.2 %collective-permute-start.3 = (bf16[768,128]{1,0:T(8,128)(2,1)S(1)}, bf16[768,128]{1,0:T(8,128)(2,1)S(1)}, u32[]{:S(2)}, u32[]{:S(2)}) collective-permute-start(bf16[768,128]{1,0:T(8,128)(2,1)S(1)} %bitcast.5), channel_id=1, source_target_pairs={{0,16},{1,17},{2,18},{3,19},{4,20},{5,21},{6,22},{7,23},{8,24},{9,... | collective-permute-start | bytes 589832 | tf_op jit(solution)/shard_map/ppermute | solution.py:35
  41.9 3.4 %collective-permute-done.3.refs_1_ = bf16[768,128]{1,0:T(8,128)(2,1)S(1)} collective-permute-done((bf16[768,128]{1,0:T(8,128)(2,1)S(1)}, bf16[768,128]{1,0:T(8,128)(2,1)S(1)}, u32[]{:S(2)}, u32[]{:S(2)}) %collective-permute-start.3) | collective-permute-done | bytes 196640 | tf_op jit(solution)/shard_map/ppermute | solution.py:35
  45.2 2.9 %all-to-all-done.1.got = bf16[4,4,2,16,768]{4,3,2,1,0:T(8,128)(2,1)S(1)} async-done(((bf16[4,4,2,16,768]{4,3,2,1,0:T(8,128)(2,1)}), bf16[4,4,2,16,768]{4,3,2,1,0:T(8,128)(2,1)S(1)}, u32[]{:S(2)}, u32[]{:S(2)}) %all-to-all-start.1) | async-done | bytes 786464 | tf_op jit(solution)/shard_map/all_to_all | solution.py:50
  48.2 1.8 %shard_map.66 = bf16[4,4,4,16,768]{4,3,2,1,0:T(8,128)(2,1)} custom-call(s32[2]{0:T(128)S(1)} %copy-done.4, bf16[4,4,2,16,768]{4,3,2,1,0:T(8,128)(2,1)S(1)} %all-to-all-done.1.got), custom_call_target="tpu_custom_call" | custom-call | bytes 3145728 | tf_op jit(solution)/shard_map/pallas_call | solution.py:144
  50.0 5.3 %all-to-all-start.2 = ((bf16[4,4,4,16,768]{4,3,2,1,0:T(8,128)(2,1)}), bf16[4,4,4,16,768]{4,3,2,1,0:T(8,128)(2,1)S(1)}, u32[]{:S(2)}, u32[]{:S(2)}) async-start(bf16[4,4,4,16,768]{4,3,2,1,0:T(8,128)(2,1)} %shard_map.66), calls=%async_computation.2 | async-start | bytes 3145728 | tf_op jit(solution)/shard_map/all_to_all | solution.py:50
  55.3 1.2 %collective-permute-start.6 = (bf16[2,768,128]{2,1,0:T(8,128)(2,1)S(1)}, bf16[2,768,128]{2,1,0:T(8,128)(2,1)S(1)}, u32[]{:S(2)}, u32[]{:S(2)}) collective-permute-start(bf16[2,768,128]{2,1,0:T(8,128)(2,1)S(1)} %shard_map.67.own), channel_id=1, source_target_pairs={{0,64},{1,65},{2,66},{3,67},{4,68},{5,69},{6,70},{7,71},{8,72},{9,... | collective-permute-start | bytes 1179656 | tf_op jit(solution)/shard_map/ppermute | solution.py:35
  56.5 0.3 collective-permute-start.5
  56.8 1.2 %collective-permute-start.4 = (bf16[2,768,128]{2,1,0:T(8,128)(2,1)S(1)}, bf16[2,768,128]{2,1,0:T(8,128)(2,1)S(1)}, u32[]{:S(2)}, u32[]{:S(2)}) collective-permute-start(bf16[2,768,128]{2,1,0:T(8,128)(2,1)S(1)} %shard_map.67.own), channel_id=1, source_target_pairs={{0,32},{1,33},{2,34},{3,35},{4,36},{5,37},{6,38},{7,39},{8,40},{9,... | collective-permute-start | bytes 1179656 | tf_op jit(solution)/shard_map/ppermute | solution.py:35
  58.0 5.9 %collective-permute-done.6.far = bf16[2,768,128]{2,1,0:T(8,128)(2,1)S(1)} collective-permute-done((bf16[2,768,128]{2,1,0:T(8,128)(2,1)S(1)}, bf16[2,768,128]{2,1,0:T(8,128)(2,1)S(1)}, u32[]{:S(2)}, u32[]{:S(2)}) %collective-permute-start.6) | collective-permute-done | bytes 393248 | tf_op jit(solution)/shard_map/ppermute | solution.py:35
  63.9 11.3 %collective-permute-done.5.above = bf16[2,768,128]{2,1,0:T(8,128)(2,1)S(1)} collective-permute-done((bf16[2,768,128]{2,1,0:T(8,128)(2,1)S(1)}, bf16[2,768,128]{2,1,0:T(8,128)(2,1)S(1)}, u32[]{:S(2)}, u32[]{:S(2)}) %collective-permute-start.5) | collective-permute-done | bytes 393248 | tf_op jit(solution)/shard_map/ppermute | solution.py:35
  75.2 1.5 %collective-permute-start.7 = (bf16[4,4,4,16,768]{4,3,2,1,0:T(8,128)(2,1)S(1)}, bf16[4,4,4,16,768]{4,3,2,1,0:T(8,128)(2,1)}, u32[]{:S(2)}, u32[]{:S(2)}) collective-permute-start(bf16[4,4,4,16,768]{4,3,2,1,0:T(8,128)(2,1)S(1)} %all-to-all-done.2.refs_3_), channel_id=1, source_target_pairs={{0,1},{1,0},{2,3},{3,2},{4,5},{5,4},{6,7},{7,6},{8,9},{9,8},{10,11... | collective-permute-start | bytes 4718600 | tf_op jit(solution)/shard_map/ppermute | solution.py:35
  76.7 0.8 dynamic-slice_subtract_fusion
  77.5 0.7 select_reduce_fusion.refs_1_
  78.1 1.6 %shard_map.68.refs_2_ = bf16[768,1024]{1,0:T(8,128)(2,1)S(1)} custom-call(s32[2]{0:T(128)S(1)} %copy-done.4, bf16[2,768,128]{2,1,0:T(8,128)(2,1)S(1)} %shard_map.67.own, bf16[2,768,128]{2,1,0:T(8,128)(2,1)S(1)} %collective-permute-done.4.below, bf16[2,768,128]{2,1,0:T(8,128)(2,1)S(1)} %collective-permute-done.5.above, ...), custom_call_target="tpu_custom_call" | custom-call | flops 402653184 | bytes 4194304 | tf_op jit(solution)/shard_map/pallas_call | solution.py:189
  79.8 1.1 copy-done
  81.0 7.5 %shard_map.69.refs_4_ = bf16[8192,1024]{1,0:T(8,128)(2,1)} custom-call(s32[2]{0:T(128)} %pad_add_fusion.pos.refs_0_, s32[64]{0:T(128)} %select_reduce_fusion.refs_1_, bf16[768,1024]{1,0:T(8,128)(2,1)} %copy-done, bf16[4,4,4,16,768]{4,3,2,1,0:T(8,128)(2,1)} %copy-done.5, bf16[4,4,4,16,768]{4,3,2,1,0:T(8,128)(2,1)} %collective-permute-done.7.refs_4_), custom_call_target="tpu_custom_call" | custom-call | flops 3221225472 | bytes 7340032 | tf_op jit(solution)/shard_map/pallas_call | solution.py:282
  88.4 3.2 %all-gather.3.cloned.1.call-done = bf16[32,4,3,16,768]{4,3,2,1,0:T(8,128)(2,1)} async-done(((bf16[4,4,3,16,768]{4,3,2,1,0:T(8,128)(2,1)}), bf16[32,4,3,16,768]{4,3,2,1,0:T(8,128)(2,1)}) %all-gather.3.cloned.1.call-update) | async-done | bytes 9437200 | tf_op jit(solution)/shard_map/all_gather | solution.py:321
  91.7 15.6 %shard_map.70 = bf16[8192,1024]{1,0:T(8,128)(2,1)} custom-call(s32[2]{0:T(128)} %pad_add_fusion.pos.refs_0_, s32[64]{0:T(128)} %select_reduce_fusion.refs_1_, bf16[768,1024]{1,0:T(8,128)(2,1)} %copy-done, bf16[8,4,4,3,16,768]{5,4,3,2,1,0:T(8,128)(2,1)} %bitcast.7, bf16[8192,1024]{1,0:T(8,128)(2,1)} %shard_map.69.refs_4_), custom_call_target="tpu_custom_call", output_to_operand_aliasing={{}: (4, {})} | custom-call | flops 9663676416 | bytes 22020096 | tf_op jit(solution)/shard_map/pallas_call | solution.py:282
  (17 shorter events, 0.1 us)
Async XLA Ops:
  11.1 7.5 %copy-start.3 = (bf16[4,2,16,768]{3,2,1,0:T(8,128)(2,1)S(1)}, bf16[4,2,16,768]{3,2,1,0:T(8,128)(2,1)}, u32[]{:S(2)}) copy-start(bf16[4,2,16,768]{3,2,1,0:T(8,128)(2,1)} %get-tuple-element.20.own) | copy-start | bytes 589828
  11.1 22.7 %copy-start.4 = (s32[2]{0:T(128)S(1)}, s32[2]{0:T(128)}, u32[]{:S(2)}) copy-start(s32[2]{0:T(128)} %pad_add_fusion.pos.refs_0_) | copy-start | bytes 28
  11.2 21.6 %all-to-all-start = ((bf16[16,3,16,768]{3,2,1,0:T(8,128)(2,1)}), bf16[16,3,16,768]{3,2,1,0:T(8,128)(2,1)S(1)}, u32[]{:S(2)}, u32[]{:S(2)}) async-start(bf16[16,3,16,768]{3,2,1,0:T(8,128)(2,1)} %get-tuple-element.21), calls=%async_computation | async-start | bytes 2359296 | tf_op jit(solution)/shard_map/all_to_all | solution.py:50
  18.6 73.1 %all-gather.3.cloned.1.call-start = ((), (), s32[]{:S(2)}) async-start(), calls=%async_computation.3 | async-start | bytes 10616832 | tf_op jit(solution)/shard_map/all_gather | solution.py:321
  18.7 6.7 %collective-permute-start.2 = (bf16[4,2,16,768]{3,2,1,0:T(8,128)(2,1)S(1)}, bf16[4,2,16,768]{3,2,1,0:T(8,128)(2,1)S(1)}, u32[]{:S(2)}, u32[]{:S(2)}) collective-permute-start(bf16[4,2,16,768]{3,2,1,0:T(8,128)(2,1)S(1)} %copy-done.3), channel_id=1, source_target_pairs={{0,8},{1,9},{2,10},{3,11},{4,12},{5,13},{6,14},{7,15},{8,0},{9,1},... | collective-permute-start | bytes 589832 | tf_op jit(solution)/shard_map/ppermute | solution.py:35
  21.7 8.9 %collective-permute-start.1 = (bf16[4,2,16,768]{3,2,1,0:T(8,128)(2,1)S(1)}, bf16[4,2,16,768]{3,2,1,0:T(8,128)(2,1)S(1)}, u32[]{:S(2)}, u32[]{:S(2)}) collective-permute-start(bf16[4,2,16,768]{3,2,1,0:T(8,128)(2,1)S(1)} %copy-done.3), channel_id=1, source_target_pairs={{0,12},{1,13},{2,14},{3,15},{4,0},{5,1},{6,2},{7,3},{8,4},{9,5},{1... | collective-permute-start | bytes 589832 | tf_op jit(solution)/shard_map/ppermute | solution.py:35
  22.4 8.2 %collective-permute-start = (bf16[4,2,16,768]{3,2,1,0:T(8,128)(2,1)S(1)}, bf16[4,2,16,768]{3,2,1,0:T(8,128)(2,1)S(1)}, u32[]{:S(2)}, u32[]{:S(2)}) collective-permute-start(bf16[4,2,16,768]{3,2,1,0:T(8,128)(2,1)S(1)} %copy-done.3), channel_id=1, source_target_pairs={{0,4},{1,5},{2,6},{3,7},{4,8},{5,9},{6,10},{7,11},{8,12},{9,13},{1... | collective-permute-start | bytes 589832 | tf_op jit(solution)/shard_map/ppermute | solution.py:35
  32.8 1.0 copy-start.6
  33.9 6.8 %copy-start.2 = (bf16[3,256,128]{2,1,0:T(8,128)(2,1)S(1)}, bf16[3,256,128]{2,1,0:T(8,128)(2,1)}, u32[]{:S(2)}) copy-start(bf16[3,256,128]{2,1,0:T(8,128)(2,1)} %param.7) | copy-start | bytes 589828
  35.4 12.8 %all-to-all-start.1 = ((bf16[4,4,2,16,768]{4,3,2,1,0:T(8,128)(2,1)}), bf16[4,4,2,16,768]{4,3,2,1,0:T(8,128)(2,1)S(1)}, u32[]{:S(2)}, u32[]{:S(2)}) async-start(bf16[4,4,2,16,768]{4,3,2,1,0:T(8,128)(2,1)} %shard_map.65), calls=%async_computation.1 | async-start | bytes 1572864 | tf_op jit(solution)/shard_map/all_to_all | solution.py:50
  40.7 4.5 %collective-permute-start.3 = (bf16[768,128]{1,0:T(8,128)(2,1)S(1)}, bf16[768,128]{1,0:T(8,128)(2,1)S(1)}, u32[]{:S(2)}, u32[]{:S(2)}) collective-permute-start(bf16[768,128]{1,0:T(8,128)(2,1)S(1)} %bitcast.5), channel_id=1, source_target_pairs={{0,16},{1,17},{2,18},{3,19},{4,20},{5,21},{6,22},{7,23},{8,24},{9,... | collective-permute-start | bytes 589832 | tf_op jit(solution)/shard_map/ppermute | solution.py:35
  50.0 28.2 %copy-start.1 = (bf16[3,256,256]{2,1,0:T(8,128)(2,1)S(1)}, bf16[3,256,256]{2,1,0:T(8,128)(2,1)}, u32[]{:S(2)}) copy-start(bf16[3,256,256]{2,1,0:T(8,128)(2,1)} %lower.1) | copy-start | bytes 1179652
  50.0 25.2 %all-to-all-start.2 = ((bf16[4,4,4,16,768]{4,3,2,1,0:T(8,128)(2,1)}), bf16[4,4,4,16,768]{4,3,2,1,0:T(8,128)(2,1)S(1)}, u32[]{:S(2)}, u32[]{:S(2)}) async-start(bf16[4,4,4,16,768]{4,3,2,1,0:T(8,128)(2,1)} %shard_map.66), calls=%async_computation.2 | async-start | bytes 3145728 | tf_op jit(solution)/shard_map/all_to_all | solution.py:50
  55.3 8.6 %collective-permute-start.6 = (bf16[2,768,128]{2,1,0:T(8,128)(2,1)S(1)}, bf16[2,768,128]{2,1,0:T(8,128)(2,1)S(1)}, u32[]{:S(2)}, u32[]{:S(2)}) collective-permute-start(bf16[2,768,128]{2,1,0:T(8,128)(2,1)S(1)} %shard_map.67.own), channel_id=1, source_target_pairs={{0,64},{1,65},{2,66},{3,67},{4,68},{5,69},{6,70},{7,71},{8,72},{9,... | collective-permute-start | bytes 1179656 | tf_op jit(solution)/shard_map/ppermute | solution.py:35
  56.5 18.7 %collective-permute-start.5 = (bf16[2,768,128]{2,1,0:T(8,128)(2,1)S(1)}, bf16[2,768,128]{2,1,0:T(8,128)(2,1)S(1)}, u32[]{:S(2)}, u32[]{:S(2)}) collective-permute-start(bf16[2,768,128]{2,1,0:T(8,128)(2,1)S(1)} %shard_map.67.own), channel_id=1, source_target_pairs={{0,96},{1,97},{2,98},{3,99},{4,100},{5,101},{6,102},{7,103},{8,104... | collective-permute-start | bytes 1179656 | tf_op jit(solution)/shard_map/ppermute | solution.py:35
  56.8 18.4 %collective-permute-start.4 = (bf16[2,768,128]{2,1,0:T(8,128)(2,1)S(1)}, bf16[2,768,128]{2,1,0:T(8,128)(2,1)S(1)}, u32[]{:S(2)}, u32[]{:S(2)}) collective-permute-start(bf16[2,768,128]{2,1,0:T(8,128)(2,1)S(1)} %shard_map.67.own), channel_id=1, source_target_pairs={{0,32},{1,33},{2,34},{3,35},{4,36},{5,37},{6,38},{7,39},{8,40},{9,... | collective-permute-start | bytes 1179656 | tf_op jit(solution)/shard_map/ppermute | solution.py:35
  75.2 4.6 %copy-start.5 = (bf16[4,4,4,16,768]{4,3,2,1,0:T(8,128)(2,1)}, bf16[4,4,4,16,768]{4,3,2,1,0:T(8,128)(2,1)S(1)}, u32[]{:S(2)}) copy-start(bf16[4,4,4,16,768]{4,3,2,1,0:T(8,128)(2,1)S(1)} %all-to-all-done.2.refs_3_) | copy-start | bytes 4718596
  75.2 5.8 %collective-permute-start.7 = (bf16[4,4,4,16,768]{4,3,2,1,0:T(8,128)(2,1)S(1)}, bf16[4,4,4,16,768]{4,3,2,1,0:T(8,128)(2,1)}, u32[]{:S(2)}, u32[]{:S(2)}) collective-permute-start(bf16[4,4,4,16,768]{4,3,2,1,0:T(8,128)(2,1)S(1)} %all-to-all-done.2.refs_3_), channel_id=1, source_target_pairs={{0,1},{1,0},{2,3},{3,2},{4,5},{5,4},{6,7},{7,6},{8,9},{9,8},{10,11... | collective-permute-start | bytes 4718600 | tf_op jit(solution)/shard_map/ppermute | solution.py:35
  79.8 1.1 %copy-start = (bf16[768,1024]{1,0:T(8,128)(2,1)}, bf16[768,1024]{1,0:T(8,128)(2,1)S(1)}, u32[]{:S(2)}) copy-start(bf16[768,1024]{1,0:T(8,128)(2,1)S(1)} %shard_map.68.refs_2_) | copy-start | bytes 4718596
Sparse Core Ops, SparseCore 0:
  34.0 57.6 all-gather.2

commit v3 on v2

--- a/solution.py
+++ b/solution.py
@@ -70,7 +70,7 @@
         c.wait()
 
 
-def solve_kernel(pos, mask, coupling, upper, a, b, c_v, u_v, hold, sem):
+def solve_kernel(mask, coupling, upper, a, b, c_v, u_v, hold, sem):
     copies = []
     for k in range(3):
         copies.append(pltpu.make_async_copy(coupling.at[k], c_v.at[k], sem.at[k, 0]))
@@ -88,20 +88,19 @@
             masked, u_v[k], (((0,), (0,)), ((), ())), preferred_element_type=F32
         )
         hold[:, :, :, k * 256 : (k + 1) * 256] = solved.astype(BF).reshape(8, 4, UR, 256)
-    x, _, z, _ = place_of(pos)
     for to in range(16):
         target = to // 4 * 2 + to % 2
         a[to] = hold[target, 0:3]
-    for dx in range(4):
-        for e in range(2):
-            b[dx, e] = hold[lax.rem(x + dx, 4) * 2 + lax.rem(z + e, 2), 3]
-
-
-def solve(pos, mask, coupling, upper):
+    for x in range(4):
+        for zl in range(2):
+            b[x, zl] = hold[x * 2 + zl, 3]
+
+
+def solve(mask, coupling, upper):
     return pl.pallas_call(
         solve_kernel,
         out_shape=(arr(16, 3, UR, KF), arr(4, 2, UR, KF)),
-        in_specs=[SM, VM, ANY, ANY],
+        in_specs=[VM, ANY, ANY],
         out_specs=(VM,) * 2,
         scratch_shapes=[
             pltpu.VMEM((3, 256, 512), BF),
@@ -111,14 +110,14 @@
         ],
         compiler_params=pltpu.CompilerParams(vmem_limit_bytes=60 << 20),
         cost_estimate=cost(2 * 512 * 256 * 768, 4 << 20),
-    )(pos, mask, coupling, upper)
+    )(mask, coupling, upper)
 
 
 def after_y_kernel(pos, own, below, above, far, out):
-    x, y, _, _ = place_of(pos)
+    _, y, _, _ = place_of(pos)
     for dy, src in ((0, own), (3, below), (1, above), (2, far)):
-        for dx in range(4):
-            out[lax.rem(x + dx, 4), lax.rem(y + dy, 4)] = src[dx]
+        for x in range(4):
+            out[x, lax.rem(y + dy, 4)] = src[x]
 
 
 def after_y(pos, *parts):
@@ -132,23 +131,22 @@
     )(pos, *parts)
 
 
-def after_x_kernel(pos, got, out):
-    _, _, z, _ = place_of(pos)
-    for x in range(4):
-        for dz in range(4):
+def after_x_kernel(got, out):
+    for z in range(4):
+        for x in range(4):
             for y in range(4):
-                out[lax.rem(z + dz, 4), x, y] = got[x, y, dz % 2]
-
-
-def after_x(pos, got):
+                out[z, x, y] = got[x, y, z % 2]
+
+
+def after_x(got):
     return pl.pallas_call(
         after_x_kernel,
         out_shape=arr(4, 4, 4, UR, KF),
-        in_specs=[SM, VM],
+        in_specs=[VM],
         out_specs=VM,
         compiler_params=pltpu.CompilerParams(vmem_limit_bytes=4 << 20),
         cost_estimate=cost(0, 3 << 20),
-    )(pos, got)
+    )(got)
 
 
 def move_kernel(where, *refs):
@@ -312,7 +310,7 @@
         jnp.where(here[None, :] == slots[:, None], slots[None, :], 0), axis=1, dtype=jnp.int32
     )
 
-    a, b = solve(pos, block_mask, coupling, upper_inverse)
+    a, b = solve(block_mask, coupling, upper_inverse)
     b_below, b_above, b_far = shift(b, dy=1), shift(b, dy=-1), shift(b, dy=2)
     own, b_below, b_above, b_far = lax.optimization_barrier(
         (exchange(a, XZ).reshape(4, 4, 3, UR, KF), b_below, b_above, b_far)
@@ -324,7 +322,7 @@
     by = after_y(pos, b, b_below, b_above, b_far)
     bx, w_other = lax.optimization_barrier((exchange(by, XX), w_other))
     pair = stack(raw, w_other)
-    bz, pair = lax.optimization_barrier((after_x(pos, bx), pair))
+    bz, pair = lax.optimization_barrier((after_x(bx), pair))
     zs = exchange(bz, ZZ)
     w_below, w_above, w_far = shift(pair, dx=1), shift(pair, dx=-1), shift(pair, dx=2)
     zs, w_below, w_above, w_far = lax.optimization_barrier((zs, w_below, w_above, w_far))

time: 116 us -> 115 us (level)
  transfers between devices with their start and end apart: 12 -> 12, of which waited for: 9 -> 9; matrix products, arithmetic and copies ran while one was open for 1% -> 1% of each run, Pallas kernels for 11% -> 10%
where the time goes in v3:
time: 115 us; the launch traced here: 113 us
  waiting for transfers between devices  37 us (32%)
  Pallas kernels  31.4 us (27%)
  starting transfers between devices  27.9 us (24%)
  between operations  13.5 us (12%)
  local copies, waits for them, and re-layouts  2.18 us (2%)
  other arithmetic  1.48 us (1%)
    ppermute x8, waiting for transfers between devices, permute(): lax.ppermute(a, AXES, [(d, linear(*to(*coords(d)))) for d in range(128)])  28.1 us
    pallas_call x2, Pallas kernels, contract(): pl.pallas_call(functools.partial(contract_kernel, groups, gathered), out_...  23 us
    all_to_all x3, starting transfers between devices, exchange(): lax.all_to_all(a, AXES, split_axis=0, concat_axis=0, tiled=True, axis_ind...  18.1 us
    ppermute x8, starting transfers between devices, permute(): lax.ppermute(a, AXES, [(d, linear(*to(*coords(d)))) for d in range(128)])  9.78 us
    all_to_all x3, waiting for transfers between devices, exchange(): lax.all_to_all(a, AXES, split_axis=0, concat_axis=0, tiled=True, axis_ind...  5.04 us
    pallas_call x1, Pallas kernels, solve(): pl.pallas_call(solve_kernel, out_shape=(arr(16, 3, UR, KF), arr(4, 2, UR,...  4.01 us
    all_gather x1, waiting for transfers between devices, local(): lax.all_gather(own, 'col', axis=0, tiled=False, axis_index_groups=YC)  3.79 us
  transfers between devices with their start and end apart: 12, of which 9 were waited for; matrix products, arithmetic and copies ran while one was open for 1% of the time, Pallas kernels for 10%

profile of v3, /device:TPU:35, one launch (start us, length us, event | category | flops | bytes accessed | tf_op | source)
XLA Modules:
  0.0 113.5 jit_solution(14927206108782358716)
XLA Ops:
  6.5 4.0 %shard_map.64 = (bf16[16,3,16,768]{3,2,1,0:T(8,128)(2,1)}, bf16[4,2,16,768]{3,2,1,0:T(8,128)(2,1)}) custom-call(s32[3,4]{1,0:T(4,128)} %mask.1, bf16[3,256,512]{2,1,0:T(8,128)(2,1)} %coupling.1, bf16[3,256,256]{2,1,0:T(8,128)(2,1)} %upper.1), custom_call_target="tpu_custom_call" | custom-call | flops 201326592 | bytes 4194304 | tf_op jit(solution)/shard_map/pallas_call | solution.py:100
  10.6 7.5 %all-to-all-start = ((bf16[16,3,16,768]{3,2,1,0:T(8,128)(2,1)}), bf16[16,3,16,768]{3,2,1,0:T(8,128)(2,1)S(1)}, u32[]{:S(2)}, u32[]{:S(2)}) async-start(bf16[16,3,16,768]{3,2,1,0:T(8,128)(2,1)} %get-tuple-element.21), calls=%async_computation | async-start | bytes 2359296 | tf_op jit(solution)/shard_map/all_to_all | solution.py:50
  18.0 0.0 all-gather.3.cloned.1.call-start
  18.1 3.0 %collective-permute-start.2 = (bf16[4,2,16,768]{3,2,1,0:T(8,128)(2,1)S(1)}, bf16[4,2,16,768]{3,2,1,0:T(8,128)(2,1)S(1)}, u32[]{:S(2)}, u32[]{:S(2)}) collective-permute-start(bf16[4,2,16,768]{3,2,1,0:T(8,128)(2,1)S(1)} %copy-done.3), channel_id=1, source_target_pairs={{0,8},{1,9},{2,10},{3,11},{4,12},{5,13},{6,14},{7,15},{8,0},{9,1},... | collective-permute-start | bytes 589832 | tf_op jit(solution)/shard_map/ppermute | solution.py:35
  21.1 0.8 collective-permute-start.1
  21.8 0.7 collective-permute-start
  22.5 2.3 %collective-permute-done.2.far = bf16[4,2,16,768]{3,2,1,0:T(8,128)(2,1)S(1)} collective-permute-done((bf16[4,2,16,768]{3,2,1,0:T(8,128)(2,1)S(1)}, bf16[4,2,16,768]{3,2,1,0:T(8,128)(2,1)S(1)}, u32[]{:S(2)}, u32[]{:S(2)}) %collective-permute-start.2) | collective-permute-done | bytes 196640 | tf_op jit(solution)/shard_map/ppermute | solution.py:35
  24.8 5.2 %collective-permute-done.1.above = bf16[4,2,16,768]{3,2,1,0:T(8,128)(2,1)S(1)} collective-permute-done((bf16[4,2,16,768]{3,2,1,0:T(8,128)(2,1)S(1)}, bf16[4,2,16,768]{3,2,1,0:T(8,128)(2,1)S(1)}, u32[]{:S(2)}, u32[]{:S(2)}) %collective-permute-start.1) | collective-permute-done | bytes 196640 | tf_op jit(solution)/shard_map/ppermute | solution.py:35
  30.0 0.1 collective-permute-done.below
  30.1 2.1 %all-to-all-done = bf16[16,3,16,768]{3,2,1,0:T(8,128)(2,1)S(1)} async-done(((bf16[16,3,16,768]{3,2,1,0:T(8,128)(2,1)}), bf16[16,3,16,768]{3,2,1,0:T(8,128)(2,1)S(1)}, u32[]{:S(2)}, u32[]{:S(2)}) %all-to-all-start) | async-done | bytes 1179680 | tf_op jit(solution)/shard_map/all_to_all | solution.py:50
  32.2 1.0 copy-done.6
  33.2 0.1 pad_add_fusion.pos.refs_0_
  33.3 1.5 %shard_map.65 = bf16[4,4,2,16,768]{4,3,2,1,0:T(8,128)(2,1)} custom-call(s32[2]{0:T(128)S(1)} %pad_add_fusion.pos.refs_0_, bf16[4,2,16,768]{3,2,1,0:T(8,128)(2,1)S(1)} %copy-done.3, bf16[4,2,16,768]{3,2,1,0:T(8,128)(2,1)S(1)} %collective-permute-done.below, bf16[4,2,16,768]{3,2,1,0:T(8,128)(2,1)S(1)} %collective-permute-done.1.above, ...), custom_call_target="tpu_custom_call" | custom-call | bytes 2097152 | tf_op jit(solution)/shard_map/pallas_call | solution.py:124
  34.8 5.3 %all-to-all-start.1 = ((bf16[4,4,2,16,768]{4,3,2,1,0:T(8,128)(2,1)}), bf16[4,4,2,16,768]{4,3,2,1,0:T(8,128)(2,1)S(1)}, u32[]{:S(2)}, u32[]{:S(2)}) async-start(bf16[4,4,2,16,768]{4,3,2,1,0:T(8,128)(2,1)} %shard_map.65), calls=%async_computation.1 | async-start | bytes 1572864 | tf_op jit(solution)/shard_map/all_to_all | solution.py:50
  40.1 1.2 %collective-permute-start.3 = (bf16[768,128]{1,0:T(8,128)(2,1)S(1)}, bf16[768,128]{1,0:T(8,128)(2,1)S(1)}, u32[]{:S(2)}, u32[]{:S(2)}) collective-permute-start(bf16[768,128]{1,0:T(8,128)(2,1)S(1)} %bitcast.5), channel_id=1, source_target_pairs={{0,16},{1,17},{2,18},{3,19},{4,20},{5,21},{6,22},{7,23},{8,24},{9,... | collective-permute-start | bytes 589832 | tf_op jit(solution)/shard_map/ppermute | solution.py:35
  41.3 3.4 %collective-permute-done.3.refs_1_ = bf16[768,128]{1,0:T(8,128)(2,1)S(1)} collective-permute-done((bf16[768,128]{1,0:T(8,128)(2,1)S(1)}, bf16[768,128]{1,0:T(8,128)(2,1)S(1)}, u32[]{:S(2)}, u32[]{:S(2)}) %collective-permute-start.3) | collective-permute-done | bytes 196640 | tf_op jit(solution)/shard_map/ppermute | solution.py:35
  44.7 2.9 %all-to-all-done.1.got = bf16[4,4,2,16,768]{4,3,2,1,0:T(8,128)(2,1)S(1)} async-done(((bf16[4,4,2,16,768]{4,3,2,1,0:T(8,128)(2,1)}), bf16[4,4,2,16,768]{4,3,2,1,0:T(8,128)(2,1)S(1)}, u32[]{:S(2)}, u32[]{:S(2)}) %all-to-all-start.1) | async-done | bytes 786464 | tf_op jit(solution)/shard_map/all_to_all | solution.py:50
  47.6 1.2 %shard_map.66 = bf16[4,4,4,16,768]{4,3,2,1,0:T(8,128)(2,1)} custom-call(bf16[4,4,2,16,768]{4,3,2,1,0:T(8,128)(2,1)S(1)} %all-to-all-done.1.got), custom_call_target="tpu_custom_call" | custom-call | bytes 3145728 | tf_op jit(solution)/shard_map/pallas_call | solution.py:142
  48.8 5.3 %all-to-all-start.2 = ((bf16[4,4,4,16,768]{4,3,2,1,0:T(8,128)(2,1)}), bf16[4,4,4,16,768]{4,3,2,1,0:T(8,128)(2,1)S(1)}, u32[]{:S(2)}, u32[]{:S(2)}) async-start(bf16[4,4,4,16,768]{4,3,2,1,0:T(8,128)(2,1)} %shard_map.66), calls=%async_computation.2 | async-start | bytes 3145728 | tf_op jit(solution)/shard_map/all_to_all | solution.py:50
  54.2 1.2 %collective-permute-start.6 = (bf16[2,768,128]{2,1,0:T(8,128)(2,1)S(1)}, bf16[2,768,128]{2,1,0:T(8,128)(2,1)S(1)}, u32[]{:S(2)}, u32[]{:S(2)}) collective-permute-start(bf16[2,768,128]{2,1,0:T(8,128)(2,1)S(1)} %shard_map.67.own), channel_id=1, source_target_pairs={{0,64},{1,65},{2,66},{3,67},{4,68},{5,69},{6,70},{7,71},{8,72},{9,... | collective-permute-start | bytes 1179656 | tf_op jit(solution)/shard_map/ppermute | solution.py:35
  55.4 0.3 collective-permute-start.5
  55.7 1.2 %collective-permute-start.4 = (bf16[2,768,128]{2,1,0:T(8,128)(2,1)S(1)}, bf16[2,768,128]{2,1,0:T(8,128)(2,1)S(1)}, u32[]{:S(2)}, u32[]{:S(2)}) collective-permute-start(bf16[2,768,128]{2,1,0:T(8,128)(2,1)S(1)} %shard_map.67.own), channel_id=1, source_target_pairs={{0,32},{1,33},{2,34},{3,35},{4,36},{5,37},{6,38},{7,39},{8,40},{9,... | collective-permute-start | bytes 1179656 | tf_op jit(solution)/shard_map/ppermute | solution.py:35
  56.8 5.9 %collective-permute-done.6.far = bf16[2,768,128]{2,1,0:T(8,128)(2,1)S(1)} collective-permute-done((bf16[2,768,128]{2,1,0:T(8,128)(2,1)S(1)}, bf16[2,768,128]{2,1,0:T(8,128)(2,1)S(1)}, u32[]{:S(2)}, u32[]{:S(2)}) %collective-permute-start.6) | collective-permute-done | bytes 393248 | tf_op jit(solution)/shard_map/ppermute | solution.py:35
  62.8 11.3 %collective-permute-done.5.above = bf16[2,768,128]{2,1,0:T(8,128)(2,1)S(1)} collective-permute-done((bf16[2,768,128]{2,1,0:T(8,128)(2,1)S(1)}, bf16[2,768,128]{2,1,0:T(8,128)(2,1)S(1)}, u32[]{:S(2)}, u32[]{:S(2)}) %collective-permute-start.5) | collective-permute-done | bytes 393248 | tf_op jit(solution)/shard_map/ppermute | solution.py:35
  74.1 1.5 %collective-permute-start.7 = (bf16[4,4,4,16,768]{4,3,2,1,0:T(8,128)(2,1)S(1)}, bf16[4,4,4,16,768]{4,3,2,1,0:T(8,128)(2,1)}, u32[]{:S(2)}, u32[]{:S(2)}) collective-permute-start(bf16[4,4,4,16,768]{4,3,2,1,0:T(8,128)(2,1)S(1)} %all-to-all-done.2.refs_3_), channel_id=1, source_target_pairs={{0,1},{1,0},{2,3},{3,2},{4,5},{5,4},{6,7},{7,6},{8,9},{9,8},{10,11... | collective-permute-start | bytes 4718600 | tf_op jit(solution)/shard_map/ppermute | solution.py:35
  75.6 0.8 dynamic-slice_subtract_fusion
  76.4 0.7 select_reduce_fusion.refs_1_
  77.0 1.6 %shard_map.68.refs_2_ = bf16[768,1024]{1,0:T(8,128)(2,1)S(1)} custom-call(s32[2]{0:T(128)S(1)} %pad_add_fusion.pos.refs_0_, bf16[2,768,128]{2,1,0:T(8,128)(2,1)S(1)} %shard_map.67.own, bf16[2,768,128]{2,1,0:T(8,128)(2,1)S(1)} %collective-permute-done.4.below, bf16[2,768,128]{2,1,0:T(8,128)(2,1)S(1)} %collective-permute-done.5.above, ...), custom_call_target="tpu_custom_call" | custom-call | flops 402653184 | bytes 4194304 | tf_op jit(solution)/shard_map/pallas_call | solution.py:187
  78.7 1.1 copy-done
  79.8 7.5 %shard_map.69.refs_4_ = bf16[8192,1024]{1,0:T(8,128)(2,1)} custom-call(s32[2]{0:T(128)} %copy-done.4, s32[64]{0:T(128)} %select_reduce_fusion.refs_1_, bf16[768,1024]{1,0:T(8,128)(2,1)} %copy-done, bf16[4,4,4,16,768]{4,3,2,1,0:T(8,128)(2,1)} %copy-done.5, bf16[4,4,4,16,768]{4,3,2,1,0:T(8,128)(2,1)} %collective-permute-done.7.refs_4_), custom_call_target="tpu_custom_call" | custom-call | flops 3221225472 | bytes 7340032 | tf_op jit(solution)/shard_map/pallas_call | solution.py:280
  87.3 3.8 %all-gather.3.cloned.1.call-done = bf16[32,4,3,16,768]{4,3,2,1,0:T(8,128)(2,1)} async-done(((bf16[4,4,3,16,768]{4,3,2,1,0:T(8,128)(2,1)}), bf16[32,4,3,16,768]{4,3,2,1,0:T(8,128)(2,1)}) %all-gather.3.cloned.1.call-update) | async-done | bytes 9437200 | tf_op jit(solution)/shard_map/all_gather | solution.py:319
  91.1 15.6 %shard_map.70 = bf16[8192,1024]{1,0:T(8,128)(2,1)} custom-call(s32[2]{0:T(128)} %copy-done.4, s32[64]{0:T(128)} %select_reduce_fusion.refs_1_, bf16[768,1024]{1,0:T(8,128)(2,1)} %copy-done, bf16[8,4,4,3,16,768]{5,4,3,2,1,0:T(8,128)(2,1)} %bitcast.7, bf16[8192,1024]{1,0:T(8,128)(2,1)} %shard_map.69.refs_4_), custom_call_target="tpu_custom_call", output_to_operand_aliasing={{}: (4, {})} | custom-call | flops 9663676416 | bytes 22020096 | tf_op jit(solution)/shard_map/pallas_call | solution.py:280
  (17 shorter events, 0.1 us)
Async XLA Ops:
  10.5 7.5 %copy-start.3 = (bf16[4,2,16,768]{3,2,1,0:T(8,128)(2,1)S(1)}, bf16[4,2,16,768]{3,2,1,0:T(8,128)(2,1)}, u32[]{:S(2)}) copy-start(bf16[4,2,16,768]{3,2,1,0:T(8,128)(2,1)} %get-tuple-element.20.own) | copy-start | bytes 589828
  10.6 21.6 %all-to-all-start = ((bf16[16,3,16,768]{3,2,1,0:T(8,128)(2,1)}), bf16[16,3,16,768]{3,2,1,0:T(8,128)(2,1)S(1)}, u32[]{:S(2)}, u32[]{:S(2)}) async-start(bf16[16,3,16,768]{3,2,1,0:T(8,128)(2,1)} %get-tuple-element.21), calls=%async_computation | async-start | bytes 2359296 | tf_op jit(solution)/shard_map/all_to_all | solution.py:50
  18.0 73.1 %all-gather.3.cloned.1.call-start = ((), (), s32[]{:S(2)}) async-start(), calls=%async_computation.3 | async-start | bytes 10616832 | tf_op jit(solution)/shard_map/all_gather | solution.py:319
  18.1 6.7 %collective-permute-start.2 = (bf16[4,2,16,768]{3,2,1,0:T(8,128)(2,1)S(1)}, bf16[4,2,16,768]{3,2,1,0:T(8,128)(2,1)S(1)}, u32[]{:S(2)}, u32[]{:S(2)}) collective-permute-start(bf16[4,2,16,768]{3,2,1,0:T(8,128)(2,1)S(1)} %copy-done.3), channel_id=1, source_target_pairs={{0,8},{1,9},{2,10},{3,11},{4,12},{5,13},{6,14},{7,15},{8,0},{9,1},... | collective-permute-start | bytes 589832 | tf_op jit(solution)/shard_map/ppermute | solution.py:35
  21.1 8.9 %collective-permute-start.1 = (bf16[4,2,16,768]{3,2,1,0:T(8,128)(2,1)S(1)}, bf16[4,2,16,768]{3,2,1,0:T(8,128)(2,1)S(1)}, u32[]{:S(2)}, u32[]{:S(2)}) collective-permute-start(bf16[4,2,16,768]{3,2,1,0:T(8,128)(2,1)S(1)} %copy-done.3), channel_id=1, source_target_pairs={{0,12},{1,13},{2,14},{3,15},{4,0},{5,1},{6,2},{7,3},{8,4},{9,5},{1... | collective-permute-start | bytes 589832 | tf_op jit(solution)/shard_map/ppermute | solution.py:35
  21.8 8.2 %collective-permute-start = (bf16[4,2,16,768]{3,2,1,0:T(8,128)(2,1)S(1)}, bf16[4,2,16,768]{3,2,1,0:T(8,128)(2,1)S(1)}, u32[]{:S(2)}, u32[]{:S(2)}) collective-permute-start(bf16[4,2,16,768]{3,2,1,0:T(8,128)(2,1)S(1)} %copy-done.3), channel_id=1, source_target_pairs={{0,4},{1,5},{2,6},{3,7},{4,8},{5,9},{6,10},{7,11},{8,12},{9,13},{1... | collective-permute-start | bytes 589832 | tf_op jit(solution)/shard_map/ppermute | solution.py:35
  32.2 1.0 copy-start.6
  33.3 43.7 %copy-start.4 = (s32[2]{0:T(128)}, s32[2]{0:T(128)S(1)}, u32[]{:S(2)}) copy-start(s32[2]{0:T(128)S(1)} %pad_add_fusion.pos.refs_0_) | copy-start | bytes 28
  33.3 6.8 %copy-start.2 = (bf16[3,256,128]{2,1,0:T(8,128)(2,1)S(1)}, bf16[3,256,128]{2,1,0:T(8,128)(2,1)}, u32[]{:S(2)}) copy-start(bf16[3,256,128]{2,1,0:T(8,128)(2,1)} %param.7) | copy-start | bytes 589828
  34.8 12.8 %all-to-all-start.1 = ((bf16[4,4,2,16,768]{4,3,2,1,0:T(8,128)(2,1)}), bf16[4,4,2,16,768]{4,3,2,1,0:T(8,128)(2,1)S(1)}, u32[]{:S(2)}, u32[]{:S(2)}) async-start(bf16[4,4,2,16,768]{4,3,2,1,0:T(8,128)(2,1)} %shard_map.65), calls=%async_computation.1 | async-start | bytes 1572864 | tf_op jit(solution)/shard_map/all_to_all | solution.py:50
  40.1 4.5 %collective-permute-start.3 = (bf16[768,128]{1,0:T(8,128)(2,1)S(1)}, bf16[768,128]{1,0:T(8,128)(2,1)S(1)}, u32[]{:S(2)}, u32[]{:S(2)}) collective-permute-start(bf16[768,128]{1,0:T(8,128)(2,1)S(1)} %bitcast.5), channel_id=1, source_target_pairs={{0,16},{1,17},{2,18},{3,19},{4,20},{5,21},{6,22},{7,23},{8,24},{9,... | collective-permute-start | bytes 589832 | tf_op jit(solution)/shard_map/ppermute | solution.py:35
  48.8 28.2 %copy-start.1 = (bf16[3,256,256]{2,1,0:T(8,128)(2,1)S(1)}, bf16[3,256,256]{2,1,0:T(8,128)(2,1)}, u32[]{:S(2)}) copy-start(bf16[3,256,256]{2,1,0:T(8,128)(2,1)} %lower.1) | copy-start | bytes 1179652
  48.8 25.2 %all-to-all-start.2 = ((bf16[4,4,4,16,768]{4,3,2,1,0:T(8,128)(2,1)}), bf16[4,4,4,16,768]{4,3,2,1,0:T(8,128)(2,1)S(1)}, u32[]{:S(2)}, u32[]{:S(2)}) async-start(bf16[4,4,4,16,768]{4,3,2,1,0:T(8,128)(2,1)} %shard_map.66), calls=%async_computation.2 | async-start | bytes 3145728 | tf_op jit(solution)/shard_map/all_to_all | solution.py:50
  54.2 8.6 %collective-permute-start.6 = (bf16[2,768,128]{2,1,0:T(8,128)(2,1)S(1)}, bf16[2,768,128]{2,1,0:T(8,128)(2,1)S(1)}, u32[]{:S(2)}, u32[]{:S(2)}) collective-permute-start(bf16[2,768,128]{2,1,0:T(8,128)(2,1)S(1)} %shard_map.67.own), channel_id=1, source_target_pairs={{0,64},{1,65},{2,66},{3,67},{4,68},{5,69},{6,70},{7,71},{8,72},{9,... | collective-permute-start | bytes 1179656 | tf_op jit(solution)/shard_map/ppermute | solution.py:35
  55.4 18.7 %collective-permute-start.5 = (bf16[2,768,128]{2,1,0:T(8,128)(2,1)S(1)}, bf16[2,768,128]{2,1,0:T(8,128)(2,1)S(1)}, u32[]{:S(2)}, u32[]{:S(2)}) collective-permute-start(bf16[2,768,128]{2,1,0:T(8,128)(2,1)S(1)} %shard_map.67.own), channel_id=1, source_target_pairs={{0,96},{1,97},{2,98},{3,99},{4,100},{5,101},{6,102},{7,103},{8,104... | collective-permute-start | bytes 1179656 | tf_op jit(solution)/shard_map/ppermute | solution.py:35
  55.7 18.4 %collective-permute-start.4 = (bf16[2,768,128]{2,1,0:T(8,128)(2,1)S(1)}, bf16[2,768,128]{2,1,0:T(8,128)(2,1)S(1)}, u32[]{:S(2)}, u32[]{:S(2)}) collective-permute-start(bf16[2,768,128]{2,1,0:T(8,128)(2,1)S(1)} %shard_map.67.own), channel_id=1, source_target_pairs={{0,32},{1,33},{2,34},{3,35},{4,36},{5,37},{6,38},{7,39},{8,40},{9,... | collective-permute-start | bytes 1179656 | tf_op jit(solution)/shard_map/ppermute | solution.py:35
  74.1 4.6 %copy-start.5 = (bf16[4,4,4,16,768]{4,3,2,1,0:T(8,128)(2,1)}, bf16[4,4,4,16,768]{4,3,2,1,0:T(8,128)(2,1)S(1)}, u32[]{:S(2)}) copy-start(bf16[4,4,4,16,768]{4,3,2,1,0:T(8,128)(2,1)S(1)} %all-to-all-done.2.refs_3_) | copy-start | bytes 4718596
  74.1 5.7 %collective-permute-start.7 = (bf16[4,4,4,16,768]{4,3,2,1,0:T(8,128)(2,1)S(1)}, bf16[4,4,4,16,768]{4,3,2,1,0:T(8,128)(2,1)}, u32[]{:S(2)}, u32[]{:S(2)}) collective-permute-start(bf16[4,4,4,16,768]{4,3,2,1,0:T(8,128)(2,1)S(1)} %all-to-all-done.2.refs_3_), channel_id=1, source_target_pairs={{0,1},{1,0},{2,3},{3,2},{4,5},{5,4},{6,7},{7,6},{8,9},{9,8},{10,11... | collective-permute-start | bytes 4718600 | tf_op jit(solution)/shard_map/ppermute | solution.py:35
  78.7 1.1 %copy-start = (bf16[768,1024]{1,0:T(8,128)(2,1)}, bf16[768,1024]{1,0:T(8,128)(2,1)S(1)}, u32[]{:S(2)}) copy-start(bf16[768,1024]{1,0:T(8,128)(2,1)S(1)} %shard_map.68.refs_2_) | copy-start | bytes 4718596
Sparse Core Ops, SparseCore 0:
  33.4 57.6 all-gather.2

commit v4 on v3

--- a/solution.py
+++ b/solution.py
@@ -11,7 +11,7 @@
 F32 = jnp.float32
 AXES = ("row", "col")
 KF = 768
-DEPTH = 3
+DEPTH = 4
 UR = 16
 ANY = pl.BlockSpec(memory_space=pl.ANY)
 VM = pl.BlockSpec(memory_space=pltpu.VMEM)
@@ -221,7 +221,7 @@
         for p in range(4):
             at = place[(groups[i] * 4 + p) * 4 + u]
             rows = pl.ds(pl.multiple_of(at * 128, 128), 128)
-            made.append(pltpu.make_async_copy(stage.at[n % 2, p], out.at[rows], out_sem.at[n % 2, p]))
+            made.append(pltpu.make_async_copy(stage.at[n % 4, p], out.at[rows], out_sem.at[n % 4, p]))
         return made
 
     for c in loads(0):
@@ -232,42 +232,46 @@
             c.start()
     right_in.wait()
     low = lax.broadcasted_iota(jnp.int32, (1, 1, 8, 256), 2) < 4
-    for n in range(len(units)):
-        for c in loads(n):
-            c.wait()
-        if n + DEPTH < len(units):
-            for c in loads(n + DEPTH):
-                c.start()
-        if n >= 2:
-            for c in stores(n - 2):
+    for n0 in range(0, len(units), 2):
+        for n in range(n0, n0 + 2):
+            for c in loads(n):
                 c.wait()
-        flat = left[n].reshape(512, KF)
+            if n + DEPTH < len(units):
+                for c in loads(n + DEPTH):
+                    c.start()
+            if n >= 4:
+                for c in stores(n - 4):
+                    c.wait()
+        flat = left[n0 : n0 + 2].reshape(2 * 512, KF)
         for j in range(4):
             cols = slice(j * 256, (j + 1) * 256)
-            acc = jnp.dot(flat, right_v[:, cols], preferred_element_type=F32)
-            if gathered:
-                acc = acc.reshape(4, 2, 4, 2, 8, 256)
-                c0, c1 = acc[:, 0].reshape(16, 2, 8, 256), acc[:, 1].reshape(16, 2, 8, 256)
-            else:
-                acc = acc.reshape(2, 16, 2, 8, 256)
-                c0, c1 = acc[0], acc[1]
-            even = jnp.where(low, c0, pltpu.roll(c1, 4, 2))
-            odd = jnp.where(low, pltpu.roll(c0, 4, 2), c1)
-            for half, made in enumerate((even, odd)):
-                for pair in range(2):
-                    for y in range(4):
-                        for zl in range(2):
-                            at = [
-                                made[y * 4 + z if gathered else z * 4 + y, pair]
-                                for z in (zl, zl + 2)
-                            ]
-                            r0 = (zl * 4 + y) * 16
-                            stage[n % 2, pair * 2 + half, r0 : r0 + 16, cols] = (
-                                jnp.concatenate(at, axis=0).astype(BF)
-                            )
-        for c in stores(n):
-            c.start()
-    for n in range(len(units) - 2, len(units)):
+            whole = jnp.dot(flat, right_v[:, cols], preferred_element_type=F32)
+            for n in range(n0, n0 + 2):
+                acc = whole[(n - n0) * 512 : (n - n0 + 1) * 512]
+                if gathered:
+                    acc = acc.reshape(4, 2, 4, 2, 8, 256)
+                    c0, c1 = acc[:, 0].reshape(16, 2, 8, 256), acc[:, 1].reshape(16, 2, 8, 256)
+                else:
+                    acc = acc.reshape(2, 16, 2, 8, 256)
+                    c0, c1 = acc[0], acc[1]
+                even = jnp.where(low, c0, pltpu.roll(c1, 4, 2))
+                odd = jnp.where(low, pltpu.roll(c0, 4, 2), c1)
+                for half, made in enumerate((even, odd)):
+                    for pair in range(2):
+                        for y in range(4):
+                            for zl in range(2):
+                                at = [
+                                    made[y * 4 + z if gathered else z * 4 + y, pair]
+                                    for z in (zl, zl + 2)
+                                ]
+                                r0 = (zl * 4 + y) * 16
+                                stage[n % 4, pair * 2 + half, r0 : r0 + 16, cols] = (
+                                    jnp.concatenate(at, axis=0).astype(BF)
+                                )
+                if j == 3:
+                    for c in stores(n):
+                        c.start()
+    for n in range(max(0, len(units) - 4), len(units)):
         for c in stores(n):
             c.wait()
 
@@ -285,10 +289,10 @@
         scratch_shapes=[
             pltpu.VMEM((KF, 1024), BF),
             pltpu.VMEM((units, 8, 4, UR, KF), BF),
-            pltpu.VMEM((2, 4, 128, 1024), BF),
+            pltpu.VMEM((4, 4, 128, 1024), BF),
             pltpu.SemaphoreType.DMA,
             pltpu.SemaphoreType.DMA((units, 2)),
-            pltpu.SemaphoreType.DMA((2, 4)),
+            pltpu.SemaphoreType.DMA((4, 4)),
         ],
         input_output_aliases={} if base is None else {len(ins) - 1: 0},
         compiler_params=pltpu.CompilerParams(vmem_limit_bytes=56 << 20),

time: 115 us -> 115 us (level)
  transfers between devices with their start and end apart: 12 -> 12, of which waited for: 9 -> 9; matrix products, arithmetic and copies ran while one was open for 1% -> 1% of each run, Pallas kernels for 10% -> 11%
where the time goes in v4:
time: 115 us; the launch traced here: 113 us
  waiting for transfers between devices  36.7 us (32%)
  Pallas kernels  31.4 us (27%)
  starting transfers between devices  27.9 us (24%)
  between operations  13.5 us (12%)
  local copies, waits for them, and re-layouts  2.18 us (2%)
  other arithmetic  1.48 us (1%)
    ppermute x8, waiting for transfers between devices, permute(): lax.ppermute(a, AXES, [(d, linear(*to(*coords(d)))) for d in range(128)])  28.1 us
    pallas_call x2, Pallas kernels, contract(): pl.pallas_call(functools.partial(contract_kernel, groups, gathered), out_...  23 us
    all_to_all x3, starting transfers between devices, exchange(): lax.all_to_all(a, AXES, split_axis=0, concat_axis=0, tiled=True, axis_ind...  18.1 us
    ppermute x8, starting transfers between devices, permute(): lax.ppermute(a, AXES, [(d, linear(*to(*coords(d)))) for d in range(128)])  9.78 us
    all_to_all x3, waiting for transfers between devices, exchange(): lax.all_to_all(a, AXES, split_axis=0, concat_axis=0, tiled=True, axis_ind...  5.04 us
    pallas_call x1, Pallas kernels, solve(): pl.pallas_call(solve_kernel, out_shape=(arr(16, 3, UR, KF), arr(4, 2, UR,...  4.01 us
    all_gather x1, waiting for transfers between devices, local(): lax.all_gather(own, 'col', axis=0, tiled=False, axis_index_groups=YC)  3.51 us
  transfers between devices with their start and end apart: 12, of which 9 were waited for; matrix products, arithmetic and copies ran while one was open for 1% of the time, Pallas kernels for 11%

profile of v4, /device:TPU:35, one launch (start us, length us, event | category | flops | bytes accessed | tf_op | source)
XLA Modules:
  0.0 113.2 jit_solution(7852113680070112716)
XLA Ops:
  6.5 4.0 %shard_map.64 = (bf16[16,3,16,768]{3,2,1,0:T(8,128)(2,1)}, bf16[4,2,16,768]{3,2,1,0:T(8,128)(2,1)}) custom-call(s32[3,4]{1,0:T(4,128)} %mask.1, bf16[3,256,512]{2,1,0:T(8,128)(2,1)} %coupling.1, bf16[3,256,256]{2,1,0:T(8,128)(2,1)} %upper.1), custom_call_target="tpu_custom_call" | custom-call | flops 201326592 | bytes 4194304 | tf_op jit(solution)/shard_map/pallas_call | solution.py:100
  10.6 7.5 %all-to-all-start = ((bf16[16,3,16,768]{3,2,1,0:T(8,128)(2,1)}), bf16[16,3,16,768]{3,2,1,0:T(8,128)(2,1)S(1)}, u32[]{:S(2)}, u32[]{:S(2)}) async-start(bf16[16,3,16,768]{3,2,1,0:T(8,128)(2,1)} %get-tuple-element.21), calls=%async_computation | async-start | bytes 2359296 | tf_op jit(solution)/shard_map/all_to_all | solution.py:50
  18.0 0.0 all-gather.3.cloned.1.call-start
  18.1 3.0 %collective-permute-start.2 = (bf16[4,2,16,768]{3,2,1,0:T(8,128)(2,1)S(1)}, bf16[4,2,16,768]{3,2,1,0:T(8,128)(2,1)S(1)}, u32[]{:S(2)}, u32[]{:S(2)}) collective-permute-start(bf16[4,2,16,768]{3,2,1,0:T(8,128)(2,1)S(1)} %copy-done.3), channel_id=1, source_target_pairs={{0,8},{1,9},{2,10},{3,11},{4,12},{5,13},{6,14},{7,15},{8,0},{9,1},... | collective-permute-start | bytes 589832 | tf_op jit(solution)/shard_map/ppermute | solution.py:35
  21.1 0.8 collective-permute-start.1
  21.8 0.7 collective-permute-start
  22.5 2.3 %collective-permute-done.2.far = bf16[4,2,16,768]{3,2,1,0:T(8,128)(2,1)S(1)} collective-permute-done((bf16[4,2,16,768]{3,2,1,0:T(8,128)(2,1)S(1)}, bf16[4,2,16,768]{3,2,1,0:T(8,128)(2,1)S(1)}, u32[]{:S(2)}, u32[]{:S(2)}) %collective-permute-start.2) | collective-permute-done | bytes 196640 | tf_op jit(solution)/shard_map/ppermute | solution.py:35
  24.8 5.2 %collective-permute-done.1.above = bf16[4,2,16,768]{3,2,1,0:T(8,128)(2,1)S(1)} collective-permute-done((bf16[4,2,16,768]{3,2,1,0:T(8,128)(2,1)S(1)}, bf16[4,2,16,768]{3,2,1,0:T(8,128)(2,1)S(1)}, u32[]{:S(2)}, u32[]{:S(2)}) %collective-permute-start.1) | collective-permute-done | bytes 196640 | tf_op jit(solution)/shard_map/ppermute | solution.py:35
  30.0 0.1 collective-permute-done.below
  30.1 2.1 %all-to-all-done = bf16[16,3,16,768]{3,2,1,0:T(8,128)(2,1)S(1)} async-done(((bf16[16,3,16,768]{3,2,1,0:T(8,128)(2,1)}), bf16[16,3,16,768]{3,2,1,0:T(8,128)(2,1)S(1)}, u32[]{:S(2)}, u32[]{:S(2)}) %all-to-all-start) | async-done | bytes 1179680 | tf_op jit(solution)/shard_map/all_to_all | solution.py:50
  32.2 1.0 copy-done.6
  33.2 0.1 pad_add_fusion.pos.refs_0_
  33.3 1.5 %shard_map.65 = bf16[4,4,2,16,768]{4,3,2,1,0:T(8,128)(2,1)} custom-call(s32[2]{0:T(128)S(1)} %pad_add_fusion.pos.refs_0_, bf16[4,2,16,768]{3,2,1,0:T(8,128)(2,1)S(1)} %copy-done.3, bf16[4,2,16,768]{3,2,1,0:T(8,128)(2,1)S(1)} %collective-permute-done.below, bf16[4,2,16,768]{3,2,1,0:T(8,128)(2,1)S(1)} %collective-permute-done.1.above, ...), custom_call_target="tpu_custom_call" | custom-call | bytes 2097152 | tf_op jit(solution)/shard_map/pallas_call | solution.py:124
  34.8 5.3 %all-to-all-start.1 = ((bf16[4,4,2,16,768]{4,3,2,1,0:T(8,128)(2,1)}), bf16[4,4,2,16,768]{4,3,2,1,0:T(8,128)(2,1)S(1)}, u32[]{:S(2)}, u32[]{:S(2)}) async-start(bf16[4,4,2,16,768]{4,3,2,1,0:T(8,128)(2,1)} %shard_map.65), calls=%async_computation.1 | async-start | bytes 1572864 | tf_op jit(solution)/shard_map/all_to_all | solution.py:50
  40.1 1.2 %collective-permute-start.3 = (bf16[768,128]{1,0:T(8,128)(2,1)S(1)}, bf16[768,128]{1,0:T(8,128)(2,1)S(1)}, u32[]{:S(2)}, u32[]{:S(2)}) collective-permute-start(bf16[768,128]{1,0:T(8,128)(2,1)S(1)} %bitcast.5), channel_id=1, source_target_pairs={{0,16},{1,17},{2,18},{3,19},{4,20},{5,21},{6,22},{7,23},{8,24},{9,... | collective-permute-start | bytes 589832 | tf_op jit(solution)/shard_map/ppermute | solution.py:35
  41.3 3.4 %collective-permute-done.3.refs_1_ = bf16[768,128]{1,0:T(8,128)(2,1)S(1)} collective-permute-done((bf16[768,128]{1,0:T(8,128)(2,1)S(1)}, bf16[768,128]{1,0:T(8,128)(2,1)S(1)}, u32[]{:S(2)}, u32[]{:S(2)}) %collective-permute-start.3) | collective-permute-done | bytes 196640 | tf_op jit(solution)/shard_map/ppermute | solution.py:35
  44.7 2.9 %all-to-all-done.1.got = bf16[4,4,2,16,768]{4,3,2,1,0:T(8,128)(2,1)S(1)} async-done(((bf16[4,4,2,16,768]{4,3,2,1,0:T(8,128)(2,1)}), bf16[4,4,2,16,768]{4,3,2,1,0:T(8,128)(2,1)S(1)}, u32[]{:S(2)}, u32[]{:S(2)}) %all-to-all-start.1) | async-done | bytes 786464 | tf_op jit(solution)/shard_map/all_to_all | solution.py:50
  47.6 1.2 %shard_map.66 = bf16[4,4,4,16,768]{4,3,2,1,0:T(8,128)(2,1)} custom-call(bf16[4,4,2,16,768]{4,3,2,1,0:T(8,128)(2,1)S(1)} %all-to-all-done.1.got), custom_call_target="tpu_custom_call" | custom-call | bytes 3145728 | tf_op jit(solution)/shard_map/pallas_call | solution.py:142
  48.8 5.3 %all-to-all-start.2 = ((bf16[4,4,4,16,768]{4,3,2,1,0:T(8,128)(2,1)}), bf16[4,4,4,16,768]{4,3,2,1,0:T(8,128)(2,1)S(1)}, u32[]{:S(2)}, u32[]{:S(2)}) async-start(bf16[4,4,4,16,768]{4,3,2,1,0:T(8,128)(2,1)} %shard_map.66), calls=%async_computation.2 | async-start | bytes 3145728 | tf_op jit(solution)/shard_map/all_to_all | solution.py:50
  54.2 1.2 %collective-permute-start.6 = (bf16[2,768,128]{2,1,0:T(8,128)(2,1)S(1)}, bf16[2,768,128]{2,1,0:T(8,128)(2,1)S(1)}, u32[]{:S(2)}, u32[]{:S(2)}) collective-permute-start(bf16[2,768,128]{2,1,0:T(8,128)(2,1)S(1)} %shard_map.67.own), channel_id=1, source_target_pairs={{0,64},{1,65},{2,66},{3,67},{4,68},{5,69},{6,70},{7,71},{8,72},{9,... | collective-permute-start | bytes 1179656 | tf_op jit(solution)/shard_map/ppermute | solution.py:35
  55.4 0.3 collective-permute-start.5
  55.7 1.2 %collective-permute-start.4 = (bf16[2,768,128]{2,1,0:T(8,128)(2,1)S(1)}, bf16[2,768,128]{2,1,0:T(8,128)(2,1)S(1)}, u32[]{:S(2)}, u32[]{:S(2)}) collective-permute-start(bf16[2,768,128]{2,1,0:T(8,128)(2,1)S(1)} %shard_map.67.own), channel_id=1, source_target_pairs={{0,32},{1,33},{2,34},{3,35},{4,36},{5,37},{6,38},{7,39},{8,40},{9,... | collective-permute-start | bytes 1179656 | tf_op jit(solution)/shard_map/ppermute | solution.py:35
  56.8 5.9 %collective-permute-done.6.far = bf16[2,768,128]{2,1,0:T(8,128)(2,1)S(1)} collective-permute-done((bf16[2,768,128]{2,1,0:T(8,128)(2,1)S(1)}, bf16[2,768,128]{2,1,0:T(8,128)(2,1)S(1)}, u32[]{:S(2)}, u32[]{:S(2)}) %collective-permute-start.6) | collective-permute-done | bytes 393248 | tf_op jit(solution)/shard_map/ppermute | solution.py:35
  62.8 11.3 %collective-permute-done.5.above = bf16[2,768,128]{2,1,0:T(8,128)(2,1)S(1)} collective-permute-done((bf16[2,768,128]{2,1,0:T(8,128)(2,1)S(1)}, bf16[2,768,128]{2,1,0:T(8,128)(2,1)S(1)}, u32[]{:S(2)}, u32[]{:S(2)}) %collective-permute-start.5) | collective-permute-done | bytes 393248 | tf_op jit(solution)/shard_map/ppermute | solution.py:35
  74.1 1.5 %collective-permute-start.7 = (bf16[4,4,4,16,768]{4,3,2,1,0:T(8,128)(2,1)S(1)}, bf16[4,4,4,16,768]{4,3,2,1,0:T(8,128)(2,1)}, u32[]{:S(2)}, u32[]{:S(2)}) collective-permute-start(bf16[4,4,4,16,768]{4,3,2,1,0:T(8,128)(2,1)S(1)} %all-to-all-done.2.refs_3_), channel_id=1, source_target_pairs={{0,1},{1,0},{2,3},{3,2},{4,5},{5,4},{6,7},{7,6},{8,9},{9,8},{10,11... | collective-permute-start | bytes 4718600 | tf_op jit(solution)/shard_map/ppermute | solution.py:35
  75.6 0.8 dynamic-slice_subtract_fusion
  76.4 0.7 select_reduce_fusion.refs_1_
  77.0 1.6 %shard_map.68.refs_2_ = bf16[768,1024]{1,0:T(8,128)(2,1)S(1)} custom-call(s32[2]{0:T(128)S(1)} %pad_add_fusion.pos.refs_0_, bf16[2,768,128]{2,1,0:T(8,128)(2,1)S(1)} %shard_map.67.own, bf16[2,768,128]{2,1,0:T(8,128)(2,1)S(1)} %collective-permute-done.4.below, bf16[2,768,128]{2,1,0:T(8,128)(2,1)S(1)} %collective-permute-done.5.above, ...), custom_call_target="tpu_custom_call" | custom-call | flops 402653184 | bytes 4194304 | tf_op jit(solution)/shard_map/pallas_call | solution.py:187
  78.7 1.1 %copy-done = bf16[768,1024]{1,0:T(8,128)(2,1)} copy-done((bf16[768,1024]{1,0:T(8,128)(2,1)}, bf16[768,1024]{1,0:T(8,128)(2,1)S(1)}, u32[]{:S(2)}) %copy-start) | copy-done | bytes 1572888
  79.8 7.8 %shard_map.69.refs_4_ = bf16[8192,1024]{1,0:T(8,128)(2,1)} custom-call(s32[2]{0:T(128)} %copy-done.4, s32[64]{0:T(128)} %select_reduce_fusion.refs_1_, bf16[768,1024]{1,0:T(8,128)(2,1)} %copy-done, bf16[4,4,4,16,768]{4,3,2,1,0:T(8,128)(2,1)} %copy-done.5, bf16[4,4,4,16,768]{4,3,2,1,0:T(8,128)(2,1)} %collective-permute-done.7.refs_4_), custom_call_target="tpu_custom_call" | custom-call | flops 3221225472 | bytes 7340032 | tf_op jit(solution)/shard_map/pallas_call | solution.py:284
  87.6 3.5 %all-gather.3.cloned.1.call-done = bf16[32,4,3,16,768]{4,3,2,1,0:T(8,128)(2,1)} async-done(((bf16[4,4,3,16,768]{4,3,2,1,0:T(8,128)(2,1)}), bf16[32,4,3,16,768]{4,3,2,1,0:T(8,128)(2,1)}) %all-gather.3.cloned.1.call-update) | async-done | bytes 9437200 | tf_op jit(solution)/shard_map/all_gather | solution.py:323
  91.1 15.2 %shard_map.70 = bf16[8192,1024]{1,0:T(8,128)(2,1)} custom-call(s32[2]{0:T(128)} %copy-done.4, s32[64]{0:T(128)} %select_reduce_fusion.refs_1_, bf16[768,1024]{1,0:T(8,128)(2,1)} %copy-done, bf16[8,4,4,3,16,768]{5,4,3,2,1,0:T(8,128)(2,1)} %bitcast.7, bf16[8192,1024]{1,0:T(8,128)(2,1)} %shard_map.69.refs_4_), custom_call_target="tpu_custom_call", output_to_operand_aliasing={{}: (4, {})} | custom-call | flops 9663676416 | bytes 22020096 | tf_op jit(solution)/shard_map/pallas_call | solution.py:284
  (17 shorter events, 0.1 us)
Async XLA Ops:
  10.5 7.5 %copy-start.3 = (bf16[4,2,16,768]{3,2,1,0:T(8,128)(2,1)S(1)}, bf16[4,2,16,768]{3,2,1,0:T(8,128)(2,1)}, u32[]{:S(2)}) copy-start(bf16[4,2,16,768]{3,2,1,0:T(8,128)(2,1)} %get-tuple-element.20.own) | copy-start | bytes 589828
  10.6 21.6 %all-to-all-start = ((bf16[16,3,16,768]{3,2,1,0:T(8,128)(2,1)}), bf16[16,3,16,768]{3,2,1,0:T(8,128)(2,1)S(1)}, u32[]{:S(2)}, u32[]{:S(2)}) async-start(bf16[16,3,16,768]{3,2,1,0:T(8,128)(2,1)} %get-tuple-element.21), calls=%async_computation | async-start | bytes 2359296 | tf_op jit(solution)/shard_map/all_to_all | solution.py:50
  18.0 73.1 %all-gather.3.cloned.1.call-start = ((), (), s32[]{:S(2)}) async-start(), calls=%async_computation.3 | async-start | bytes 10616832 | tf_op jit(solution)/shard_map/all_gather | solution.py:323
  18.1 6.7 %collective-permute-start.2 = (bf16[4,2,16,768]{3,2,1,0:T(8,128)(2,1)S(1)}, bf16[4,2,16,768]{3,2,1,0:T(8,128)(2,1)S(1)}, u32[]{:S(2)}, u32[]{:S(2)}) collective-permute-start(bf16[4,2,16,768]{3,2,1,0:T(8,128)(2,1)S(1)} %copy-done.3), channel_id=1, source_target_pairs={{0,8},{1,9},{2,10},{3,11},{4,12},{5,13},{6,14},{7,15},{8,0},{9,1},... | collective-permute-start | bytes 589832 | tf_op jit(solution)/shard_map/ppermute | solution.py:35
  21.1 8.9 %collective-permute-start.1 = (bf16[4,2,16,768]{3,2,1,0:T(8,128)(2,1)S(1)}, bf16[4,2,16,768]{3,2,1,0:T(8,128)(2,1)S(1)}, u32[]{:S(2)}, u32[]{:S(2)}) collective-permute-start(bf16[4,2,16,768]{3,2,1,0:T(8,128)(2,1)S(1)} %copy-done.3), channel_id=1, source_target_pairs={{0,12},{1,13},{2,14},{3,15},{4,0},{5,1},{6,2},{7,3},{8,4},{9,5},{1... | collective-permute-start | bytes 589832 | tf_op jit(solution)/shard_map/ppermute | solution.py:35
  21.8 8.2 %collective-permute-start = (bf16[4,2,16,768]{3,2,1,0:T(8,128)(2,1)S(1)}, bf16[4,2,16,768]{3,2,1,0:T(8,128)(2,1)S(1)}, u32[]{:S(2)}, u32[]{:S(2)}) collective-permute-start(bf16[4,2,16,768]{3,2,1,0:T(8,128)(2,1)S(1)} %copy-done.3), channel_id=1, source_target_pairs={{0,4},{1,5},{2,6},{3,7},{4,8},{5,9},{6,10},{7,11},{8,12},{9,13},{1... | collective-permute-start | bytes 589832 | tf_op jit(solution)/shard_map/ppermute | solution.py:35
  32.2 1.0 copy-start.6
  33.3 43.7 %copy-start.4 = (s32[2]{0:T(128)}, s32[2]{0:T(128)S(1)}, u32[]{:S(2)}) copy-start(s32[2]{0:T(128)S(1)} %pad_add_fusion.pos.refs_0_) | copy-start | bytes 28
  33.3 6.8 %copy-start.2 = (bf16[3,256,128]{2,1,0:T(8,128)(2,1)S(1)}, bf16[3,256,128]{2,1,0:T(8,128)(2,1)}, u32[]{:S(2)}) copy-start(bf16[3,256,128]{2,1,0:T(8,128)(2,1)} %param.7) | copy-start | bytes 589828
  34.8 12.8 %all-to-all-start.1 = ((bf16[4,4,2,16,768]{4,3,2,1,0:T(8,128)(2,1)}), bf16[4,4,2,16,768]{4,3,2,1,0:T(8,128)(2,1)S(1)}, u32[]{:S(2)}, u32[]{:S(2)}) async-start(bf16[4,4,2,16,768]{4,3,2,1,0:T(8,128)(2,1)} %shard_map.65), calls=%async_computation.1 | async-start | bytes 1572864 | tf_op jit(solution)/shard_map/all_to_all | solution.py:50
  40.1 4.5 %collective-permute-start.3 = (bf16[768,128]{1,0:T(8,128)(2,1)S(1)}, bf16[768,128]{1,0:T(8,128)(2,1)S(1)}, u32[]{:S(2)}, u32[]{:S(2)}) collective-permute-start(bf16[768,128]{1,0:T(8,128)(2,1)S(1)} %bitcast.5), channel_id=1, source_target_pairs={{0,16},{1,17},{2,18},{3,19},{4,20},{5,21},{6,22},{7,23},{8,24},{9,... | collective-permute-start | bytes 589832 | tf_op jit(solution)/shard_map/ppermute | solution.py:35
  48.8 28.2 %copy-start.1 = (bf16[3,256,256]{2,1,0:T(8,128)(2,1)S(1)}, bf16[3,256,256]{2,1,0:T(8,128)(2,1)}, u32[]{:S(2)}) copy-start(bf16[3,256,256]{2,1,0:T(8,128)(2,1)} %lower.1) | copy-start | bytes 1179652
  48.8 25.2 %all-to-all-start.2 = ((bf16[4,4,4,16,768]{4,3,2,1,0:T(8,128)(2,1)}), bf16[4,4,4,16,768]{4,3,2,1,0:T(8,128)(2,1)S(1)}, u32[]{:S(2)}, u32[]{:S(2)}) async-start(bf16[4,4,4,16,768]{4,3,2,1,0:T(8,128)(2,1)} %shard_map.66), calls=%async_computation.2 | async-start | bytes 3145728 | tf_op jit(solution)/shard_map/all_to_all | solution.py:50
  54.2 8.6 %collective-permute-start.6 = (bf16[2,768,128]{2,1,0:T(8,128)(2,1)S(1)}, bf16[2,768,128]{2,1,0:T(8,128)(2,1)S(1)}, u32[]{:S(2)}, u32[]{:S(2)}) collective-permute-start(bf16[2,768,128]{2,1,0:T(8,128)(2,1)S(1)} %shard_map.67.own), channel_id=1, source_target_pairs={{0,64},{1,65},{2,66},{3,67},{4,68},{5,69},{6,70},{7,71},{8,72},{9,... | collective-permute-start | bytes 1179656 | tf_op jit(solution)/shard_map/ppermute | solution.py:35
  55.4 18.7 %collective-permute-start.5 = (bf16[2,768,128]{2,1,0:T(8,128)(2,1)S(1)}, bf16[2,768,128]{2,1,0:T(8,128)(2,1)S(1)}, u32[]{:S(2)}, u32[]{:S(2)}) collective-permute-start(bf16[2,768,128]{2,1,0:T(8,128)(2,1)S(1)} %shard_map.67.own), channel_id=1, source_target_pairs={{0,96},{1,97},{2,98},{3,99},{4,100},{5,101},{6,102},{7,103},{8,104... | collective-permute-start | bytes 1179656 | tf_op jit(solution)/shard_map/ppermute | solution.py:35
  55.7 18.4 %collective-permute-start.4 = (bf16[2,768,128]{2,1,0:T(8,128)(2,1)S(1)}, bf16[2,768,128]{2,1,0:T(8,128)(2,1)S(1)}, u32[]{:S(2)}, u32[]{:S(2)}) collective-permute-start(bf16[2,768,128]{2,1,0:T(8,128)(2,1)S(1)} %shard_map.67.own), channel_id=1, source_target_pairs={{0,32},{1,33},{2,34},{3,35},{4,36},{5,37},{6,38},{7,39},{8,40},{9,... | collective-permute-start | bytes 1179656 | tf_op jit(solution)/shard_map/ppermute | solution.py:35
  74.1 4.6 %copy-start.5 = (bf16[4,4,4,16,768]{4,3,2,1,0:T(8,128)(2,1)}, bf16[4,4,4,16,768]{4,3,2,1,0:T(8,128)(2,1)S(1)}, u32[]{:S(2)}) copy-start(bf16[4,4,4,16,768]{4,3,2,1,0:T(8,128)(2,1)S(1)} %all-to-all-done.2.refs_3_) | copy-start | bytes 4718596
  74.1 5.7 %collective-permute-start.7 = (bf16[4,4,4,16,768]{4,3,2,1,0:T(8,128)(2,1)S(1)}, bf16[4,4,4,16,768]{4,3,2,1,0:T(8,128)(2,1)}, u32[]{:S(2)}, u32[]{:S(2)}) collective-permute-start(bf16[4,4,4,16,768]{4,3,2,1,0:T(8,128)(2,1)S(1)} %all-to-all-done.2.refs_3_), channel_id=1, source_target_pairs={{0,1},{1,0},{2,3},{3,2},{4,5},{5,4},{6,7},{7,6},{8,9},{9,8},{10,11... | collective-permute-start | bytes 4718600 | tf_op jit(solution)/shard_map/ppermute | solution.py:35
  78.7 1.1 %copy-start = (bf16[768,1024]{1,0:T(8,128)(2,1)}, bf16[768,1024]{1,0:T(8,128)(2,1)S(1)}, u32[]{:S(2)}) copy-start(bf16[768,1024]{1,0:T(8,128)(2,1)S(1)} %shard_map.68.refs_2_) | copy-start | bytes 4718596
Sparse Core Ops, SparseCore 0:
  33.4 57.6 all-gather.2

commit v5 on v4

--- a/solution.py
+++ b/solution.py
@@ -215,13 +215,20 @@
             pltpu.make_async_copy(src, dst, in_sem.at[n, k]) for k, (src, dst) in enumerate(pairs)
         ]
 
-    def stores(n):
+    def stores(n, cols=slice(0, 1024)):
         u, i = units[n]
         made = []
+        span = pl.ds(cols.start, cols.stop - cols.start)
         for p in range(4):
             at = place[(groups[i] * 4 + p) * 4 + u]
             rows = pl.ds(pl.multiple_of(at * 128, 128), 128)
-            made.append(pltpu.make_async_copy(stage.at[n % 4, p], out.at[rows], out_sem.at[n % 4, p]))
+            made.append(
+                pltpu.make_async_copy(
+                    stage.at[n % 4, p, :, span],
+                    out.at[rows, span],
+                    out_sem.at[n % 4, p, cols.start // 256],
+                )
+            )
         return made
 
     for c in loads(0):
@@ -268,12 +275,19 @@
                                 stage[n % 4, pair * 2 + half, r0 : r0 + 16, cols] = (
                                     jnp.concatenate(at, axis=0).astype(BF)
                                 )
-                if j == 3:
+                if n >= len(units) - 2:
+                    for c in stores(n, cols):
+                        c.start()
+                elif j == 3:
                     for c in stores(n):
                         c.start()
-    for n in range(max(0, len(units) - 4), len(units)):
+    for n in range(len(units) - 4, len(units) - 2):
         for c in stores(n):
             c.wait()
+    for n in range(len(units) - 2, len(units)):
+        for j in range(4):
+            for c in stores(n, slice(j * 256, (j + 1) * 256)):
+                c.wait()
 
 
 def contract(groups, gathered, pos, place, right, parts, base):
@@ -292,7 +306,7 @@
             pltpu.VMEM((4, 4, 128, 1024), BF),
             pltpu.SemaphoreType.DMA,
             pltpu.SemaphoreType.DMA((units, 2)),
-            pltpu.SemaphoreType.DMA((4, 4)),
+            pltpu.SemaphoreType.DMA((4, 4, 4)),
         ],
         input_output_aliases={} if base is None else {len(ins) - 1: 0},
         compiler_params=pltpu.CompilerParams(vmem_limit_bytes=56 << 20),

time: 115 us -> 115 us (level)
  no operation moved by 1% of the time
where the time goes in v5:
time: 115 us; the launch traced here: 113 us
  waiting for transfers between devices  36.6 us (32%)
  Pallas kernels  31.5 us (27%)
  starting transfers between devices  27.9 us (24%)
  between operations  13.5 us (12%)
  local copies, waits for them, and re-layouts  2.18 us (2%)
  other arithmetic  1.48 us (1%)
    ppermute x8, waiting for transfers between devices, permute(): lax.ppermute(a, AXES, [(d, linear(*to(*coords(d)))) for d in range(128)])  28.1 us
    pallas_call x2, Pallas kernels, contract(): pl.pallas_call(functools.partial(contract_kernel, groups, gathered), out_...  23.1 us
    all_to_all x3, starting transfers between devices, exchange(): lax.all_to_all(a, AXES, split_axis=0, concat_axis=0, tiled=True, axis_ind...  18.1 us
    ppermute x8, starting transfers between devices, permute(): lax.ppermute(a, AXES, [(d, linear(*to(*coords(d)))) for d in range(128)])  9.78 us
    all_to_all x3, waiting for transfers between devices, exchange(): lax.all_to_all(a, AXES, split_axis=0, concat_axis=0, tiled=True, axis_ind...  5.04 us
    pallas_call x1, Pallas kernels, solve(): pl.pallas_call(solve_kernel, out_shape=(arr(16, 3, UR, KF), arr(4, 2, UR,...  4.01 us
    all_gather x1, waiting for transfers between devices, local(): lax.all_gather(own, 'col', axis=0, tiled=False, axis_index_groups=YC)  3.43 us
  transfers between devices with their start and end apart: 12, of which 9 were waited for; matrix products, arithmetic and copies ran while one was open for 1% of the time, Pallas kernels for 11%

profile of v5, /device:TPU:35, one launch (start us, length us, event | category | flops | bytes accessed | tf_op | source)
XLA Modules:
  0.0 113.3 jit_solution(11751407106940246827)
XLA Ops:
  6.5 4.0 %shard_map.64 = (bf16[16,3,16,768]{3,2,1,0:T(8,128)(2,1)}, bf16[4,2,16,768]{3,2,1,0:T(8,128)(2,1)}) custom-call(s32[3,4]{1,0:T(4,128)} %mask.1, bf16[3,256,512]{2,1,0:T(8,128)(2,1)} %coupling.1, bf16[3,256,256]{2,1,0:T(8,128)(2,1)} %upper.1), custom_call_target="tpu_custom_call" | custom-call | flops 201326592 | bytes 4194304 | tf_op jit(solution)/shard_map/pallas_call | solution.py:100
  10.6 7.5 %all-to-all-start = ((bf16[16,3,16,768]{3,2,1,0:T(8,128)(2,1)}), bf16[16,3,16,768]{3,2,1,0:T(8,128)(2,1)S(1)}, u32[]{:S(2)}, u32[]{:S(2)}) async-start(bf16[16,3,16,768]{3,2,1,0:T(8,128)(2,1)} %get-tuple-element.21), calls=%async_computation | async-start | bytes 2359296 | tf_op jit(solution)/shard_map/all_to_all | solution.py:50
  18.0 0.0 all-gather.3.cloned.1.call-start
  18.1 3.0 %collective-permute-start.2 = (bf16[4,2,16,768]{3,2,1,0:T(8,128)(2,1)S(1)}, bf16[4,2,16,768]{3,2,1,0:T(8,128)(2,1)S(1)}, u32[]{:S(2)}, u32[]{:S(2)}) collective-permute-start(bf16[4,2,16,768]{3,2,1,0:T(8,128)(2,1)S(1)} %copy-done.3), channel_id=1, source_target_pairs={{0,8},{1,9},{2,10},{3,11},{4,12},{5,13},{6,14},{7,15},{8,0},{9,1},... | collective-permute-start | bytes 589832 | tf_op jit(solution)/shard_map/ppermute | solution.py:35
  21.1 0.8 collective-permute-start.1
  21.8 0.7 collective-permute-start
  22.5 2.3 %collective-permute-done.2.far = bf16[4,2,16,768]{3,2,1,0:T(8,128)(2,1)S(1)} collective-permute-done((bf16[4,2,16,768]{3,2,1,0:T(8,128)(2,1)S(1)}, bf16[4,2,16,768]{3,2,1,0:T(8,128)(2,1)S(1)}, u32[]{:S(2)}, u32[]{:S(2)}) %collective-permute-start.2) | collective-permute-done | bytes 196640 | tf_op jit(solution)/shard_map/ppermute | solution.py:35
  24.8 5.2 %collective-permute-done.1.above = bf16[4,2,16,768]{3,2,1,0:T(8,128)(2,1)S(1)} collective-permute-done((bf16[4,2,16,768]{3,2,1,0:T(8,128)(2,1)S(1)}, bf16[4,2,16,768]{3,2,1,0:T(8,128)(2,1)S(1)}, u32[]{:S(2)}, u32[]{:S(2)}) %collective-permute-start.1) | collective-permute-done | bytes 196640 | tf_op jit(solution)/shard_map/ppermute | solution.py:35
  30.0 0.1 collective-permute-done.below
  30.1 2.1 %all-to-all-done = bf16[16,3,16,768]{3,2,1,0:T(8,128)(2,1)S(1)} async-done(((bf16[16,3,16,768]{3,2,1,0:T(8,128)(2,1)}), bf16[16,3,16,768]{3,2,1,0:T(8,128)(2,1)S(1)}, u32[]{:S(2)}, u32[]{:S(2)}) %all-to-all-start) | async-done | bytes 1179680 | tf_op jit(solution)/shard_map/all_to_all | solution.py:50
  32.2 1.0 copy-done.6
  33.2 0.1 pad_add_fusion.pos.refs_0_
  33.3 1.5 %shard_map.65 = bf16[4,4,2,16,768]{4,3,2,1,0:T(8,128)(2,1)} custom-call(s32[2]{0:T(128)S(1)} %pad_add_fusion.pos.refs_0_, bf16[4,2,16,768]{3,2,1,0:T(8,128)(2,1)S(1)} %copy-done.3, bf16[4,2,16,768]{3,2,1,0:T(8,128)(2,1)S(1)} %collective-permute-done.below, bf16[4,2,16,768]{3,2,1,0:T(8,128)(2,1)S(1)} %collective-permute-done.1.above, ...), custom_call_target="tpu_custom_call" | custom-call | bytes 2097152 | tf_op jit(solution)/shard_map/pallas_call | solution.py:124
  34.8 5.3 %all-to-all-start.1 = ((bf16[4,4,2,16,768]{4,3,2,1,0:T(8,128)(2,1)}), bf16[4,4,2,16,768]{4,3,2,1,0:T(8,128)(2,1)S(1)}, u32[]{:S(2)}, u32[]{:S(2)}) async-start(bf16[4,4,2,16,768]{4,3,2,1,0:T(8,128)(2,1)} %shard_map.65), calls=%async_computation.1 | async-start | bytes 1572864 | tf_op jit(solution)/shard_map/all_to_all | solution.py:50
  40.1 1.2 %collective-permute-start.3 = (bf16[768,128]{1,0:T(8,128)(2,1)S(1)}, bf16[768,128]{1,0:T(8,128)(2,1)S(1)}, u32[]{:S(2)}, u32[]{:S(2)}) collective-permute-start(bf16[768,128]{1,0:T(8,128)(2,1)S(1)} %bitcast.5), channel_id=1, source_target_pairs={{0,16},{1,17},{2,18},{3,19},{4,20},{5,21},{6,22},{7,23},{8,24},{9,... | collective-permute-start | bytes 589832 | tf_op jit(solution)/shard_map/ppermute | solution.py:35
  41.3 3.4 %collective-permute-done.3.refs_1_ = bf16[768,128]{1,0:T(8,128)(2,1)S(1)} collective-permute-done((bf16[768,128]{1,0:T(8,128)(2,1)S(1)}, bf16[768,128]{1,0:T(8,128)(2,1)S(1)}, u32[]{:S(2)}, u32[]{:S(2)}) %collective-permute-start.3) | collective-permute-done | bytes 196640 | tf_op jit(solution)/shard_map/ppermute | solution.py:35
  44.7 2.9 %all-to-all-done.1.got = bf16[4,4,2,16,768]{4,3,2,1,0:T(8,128)(2,1)S(1)} async-done(((bf16[4,4,2,16,768]{4,3,2,1,0:T(8,128)(2,1)}), bf16[4,4,2,16,768]{4,3,2,1,0:T(8,128)(2,1)S(1)}, u32[]{:S(2)}, u32[]{:S(2)}) %all-to-all-start.1) | async-done | bytes 786464 | tf_op jit(solution)/shard_map/all_to_all | solution.py:50
  47.6 1.2 %shard_map.66 = bf16[4,4,4,16,768]{4,3,2,1,0:T(8,128)(2,1)} custom-call(bf16[4,4,2,16,768]{4,3,2,1,0:T(8,128)(2,1)S(1)} %all-to-all-done.1.got), custom_call_target="tpu_custom_call" | custom-call | bytes 3145728 | tf_op jit(solution)/shard_map/pallas_call | solution.py:142
  48.8 5.3 %all-to-all-start.2 = ((bf16[4,4,4,16,768]{4,3,2,1,0:T(8,128)(2,1)}), bf16[4,4,4,16,768]{4,3,2,1,0:T(8,128)(2,1)S(1)}, u32[]{:S(2)}, u32[]{:S(2)}) async-start(bf16[4,4,4,16,768]{4,3,2,1,0:T(8,128)(2,1)} %shard_map.66), calls=%async_computation.2 | async-start | bytes 3145728 | tf_op jit(solution)/shard_map/all_to_all | solution.py:50
  54.2 1.2 %collective-permute-start.6 = (bf16[2,768,128]{2,1,0:T(8,128)(2,1)S(1)}, bf16[2,768,128]{2,1,0:T(8,128)(2,1)S(1)}, u32[]{:S(2)}, u32[]{:S(2)}) collective-permute-start(bf16[2,768,128]{2,1,0:T(8,128)(2,1)S(1)} %shard_map.67.own), channel_id=1, source_target_pairs={{0,64},{1,65},{2,66},{3,67},{4,68},{5,69},{6,70},{7,71},{8,72},{9,... | collective-permute-start | bytes 1179656 | tf_op jit(solution)/shard_map/ppermute | solution.py:35
  55.4 0.3 collective-permute-start.5
  55.7 1.2 %collective-permute-start.4 = (bf16[2,768,128]{2,1,0:T(8,128)(2,1)S(1)}, bf16[2,768,128]{2,1,0:T(8,128)(2,1)S(1)}, u32[]{:S(2)}, u32[]{:S(2)}) collective-permute-start(bf16[2,768,128]{2,1,0:T(8,128)(2,1)S(1)} %shard_map.67.own), channel_id=1, source_target_pairs={{0,32},{1,33},{2,34},{3,35},{4,36},{5,37},{6,38},{7,39},{8,40},{9,... | collective-permute-start | bytes 1179656 | tf_op jit(solution)/shard_map/ppermute | solution.py:35
  56.8 5.9 %collective-permute-done.6.far = bf16[2,768,128]{2,1,0:T(8,128)(2,1)S(1)} collective-permute-done((bf16[2,768,128]{2,1,0:T(8,128)(2,1)S(1)}, bf16[2,768,128]{2,1,0:T(8,128)(2,1)S(1)}, u32[]{:S(2)}, u32[]{:S(2)}) %collective-permute-start.6) | collective-permute-done | bytes 393248 | tf_op jit(solution)/shard_map/ppermute | solution.py:35
  62.8 11.3 %collective-permute-done.5.above = bf16[2,768,128]{2,1,0:T(8,128)(2,1)S(1)} collective-permute-done((bf16[2,768,128]{2,1,0:T(8,128)(2,1)S(1)}, bf16[2,768,128]{2,1,0:T(8,128)(2,1)S(1)}, u32[]{:S(2)}, u32[]{:S(2)}) %collective-permute-start.5) | collective-permute-done | bytes 393248 | tf_op jit(solution)/shard_map/ppermute | solution.py:35
  74.1 1.5 %collective-permute-start.7 = (bf16[4,4,4,16,768]{4,3,2,1,0:T(8,128)(2,1)S(1)}, bf16[4,4,4,16,768]{4,3,2,1,0:T(8,128)(2,1)}, u32[]{:S(2)}, u32[]{:S(2)}) collective-permute-start(bf16[4,4,4,16,768]{4,3,2,1,0:T(8,128)(2,1)S(1)} %all-to-all-done.2.refs_3_), channel_id=1, source_target_pairs={{0,1},{1,0},{2,3},{3,2},{4,5},{5,4},{6,7},{7,6},{8,9},{9,8},{10,11... | collective-permute-start | bytes 4718600 | tf_op jit(solution)/shard_map/ppermute | solution.py:35
  75.6 0.8 dynamic-slice_subtract_fusion
  76.4 0.7 select_reduce_fusion.refs_1_
  77.0 1.6 %shard_map.68.refs_2_ = bf16[768,1024]{1,0:T(8,128)(2,1)S(1)} custom-call(s32[2]{0:T(128)S(1)} %pad_add_fusion.pos.refs_0_, bf16[2,768,128]{2,1,0:T(8,128)(2,1)S(1)} %shard_map.67.own, bf16[2,768,128]{2,1,0:T(8,128)(2,1)S(1)} %collective-permute-done.4.below, bf16[2,768,128]{2,1,0:T(8,128)(2,1)S(1)} %collective-permute-done.5.above, ...), custom_call_target="tpu_custom_call" | custom-call | flops 402653184 | bytes 4194304 | tf_op jit(solution)/shard_map/pallas_call | solution.py:187
  78.7 1.1 %copy-done = bf16[768,1024]{1,0:T(8,128)(2,1)} copy-done((bf16[768,1024]{1,0:T(8,128)(2,1)}, bf16[768,1024]{1,0:T(8,128)(2,1)S(1)}, u32[]{:S(2)}) %copy-start) | copy-done | bytes 1572888
  79.8 7.8 %shard_map.69.refs_4_ = bf16[8192,1024]{1,0:T(8,128)(2,1)} custom-call(s32[2]{0:T(128)} %copy-done.4, s32[64]{0:T(128)} %select_reduce_fusion.refs_1_, bf16[768,1024]{1,0:T(8,128)(2,1)} %copy-done, bf16[4,4,4,16,768]{4,3,2,1,0:T(8,128)(2,1)} %copy-done.5, bf16[4,4,4,16,768]{4,3,2,1,0:T(8,128)(2,1)} %collective-permute-done.7.refs_4_), custom_call_target="tpu_custom_call" | custom-call | flops 3221225472 | bytes 7340032 | tf_op jit(solution)/shard_map/pallas_call | solution.py:298
  87.6 3.4 %all-gather.3.cloned.1.call-done = bf16[32,4,3,16,768]{4,3,2,1,0:T(8,128)(2,1)} async-done(((bf16[4,4,3,16,768]{4,3,2,1,0:T(8,128)(2,1)}), bf16[32,4,3,16,768]{4,3,2,1,0:T(8,128)(2,1)}) %all-gather.3.cloned.1.call-update) | async-done | bytes 9437200 | tf_op jit(solution)/shard_map/all_gather | solution.py:337
  91.1 15.3 %shard_map.70 = bf16[8192,1024]{1,0:T(8,128)(2,1)} custom-call(s32[2]{0:T(128)} %copy-done.4, s32[64]{0:T(128)} %select_reduce_fusion.refs_1_, bf16[768,1024]{1,0:T(8,128)(2,1)} %copy-done, bf16[8,4,4,3,16,768]{5,4,3,2,1,0:T(8,128)(2,1)} %bitcast.7, bf16[8192,1024]{1,0:T(8,128)(2,1)} %shard_map.69.refs_4_), custom_call_target="tpu_custom_call", output_to_operand_aliasing={{}: (4, {})} | custom-call | flops 9663676416 | bytes 22020096 | tf_op jit(solution)/shard_map/pallas_call | solution.py:298
  (17 shorter events, 0.1 us)
Async XLA Ops:
  10.5 7.5 %copy-start.3 = (bf16[4,2,16,768]{3,2,1,0:T(8,128)(2,1)S(1)}, bf16[4,2,16,768]{3,2,1,0:T(8,128)(2,1)}, u32[]{:S(2)}) copy-start(bf16[4,2,16,768]{3,2,1,0:T(8,128)(2,1)} %get-tuple-element.20.own) | copy-start | bytes 589828
  10.6 21.6 %all-to-all-start = ((bf16[16,3,16,768]{3,2,1,0:T(8,128)(2,1)}), bf16[16,3,16,768]{3,2,1,0:T(8,128)(2,1)S(1)}, u32[]{:S(2)}, u32[]{:S(2)}) async-start(bf16[16,3,16,768]{3,2,1,0:T(8,128)(2,1)} %get-tuple-element.21), calls=%async_computation | async-start | bytes 2359296 | tf_op jit(solution)/shard_map/all_to_all | solution.py:50
  18.0 73.1 %all-gather.3.cloned.1.call-start = ((), (), s32[]{:S(2)}) async-start(), calls=%async_computation.3 | async-start | bytes 10616832 | tf_op jit(solution)/shard_map/all_gather | solution.py:337
  18.1 6.7 %collective-permute-start.2 = (bf16[4,2,16,768]{3,2,1,0:T(8,128)(2,1)S(1)}, bf16[4,2,16,768]{3,2,1,0:T(8,128)(2,1)S(1)}, u32[]{:S(2)}, u32[]{:S(2)}) collective-permute-start(bf16[4,2,16,768]{3,2,1,0:T(8,128)(2,1)S(1)} %copy-done.3), channel_id=1, source_target_pairs={{0,8},{1,9},{2,10},{3,11},{4,12},{5,13},{6,14},{7,15},{8,0},{9,1},... | collective-permute-start | bytes 589832 | tf_op jit(solution)/shard_map/ppermute | solution.py:35
  21.1 8.9 %collective-permute-start.1 = (bf16[4,2,16,768]{3,2,1,0:T(8,128)(2,1)S(1)}, bf16[4,2,16,768]{3,2,1,0:T(8,128)(2,1)S(1)}, u32[]{:S(2)}, u32[]{:S(2)}) collective-permute-start(bf16[4,2,16,768]{3,2,1,0:T(8,128)(2,1)S(1)} %copy-done.3), channel_id=1, source_target_pairs={{0,12},{1,13},{2,14},{3,15},{4,0},{5,1},{6,2},{7,3},{8,4},{9,5},{1... | collective-permute-start | bytes 589832 | tf_op jit(solution)/shard_map/ppermute | solution.py:35
  21.8 8.2 %collective-permute-start = (bf16[4,2,16,768]{3,2,1,0:T(8,128)(2,1)S(1)}, bf16[4,2,16,768]{3,2,1,0:T(8,128)(2,1)S(1)}, u32[]{:S(2)}, u32[]{:S(2)}) collective-permute-start(bf16[4,2,16,768]{3,2,1,0:T(8,128)(2,1)S(1)} %copy-done.3), channel_id=1, source_target_pairs={{0,4},{1,5},{2,6},{3,7},{4,8},{5,9},{6,10},{7,11},{8,12},{9,13},{1... | collective-permute-start | bytes 589832 | tf_op jit(solution)/shard_map/ppermute | solution.py:35
  32.2 1.0 copy-start.6
  33.3 43.7 %copy-start.4 = (s32[2]{0:T(128)}, s32[2]{0:T(128)S(1)}, u32[]{:S(2)}) copy-start(s32[2]{0:T(128)S(1)} %pad_add_fusion.pos.refs_0_) | copy-start | bytes 28
  33.3 6.8 %copy-start.2 = (bf16[3,256,128]{2,1,0:T(8,128)(2,1)S(1)}, bf16[3,256,128]{2,1,0:T(8,128)(2,1)}, u32[]{:S(2)}) copy-start(bf16[3,256,128]{2,1,0:T(8,128)(2,1)} %param.7) | copy-start | bytes 589828
  34.8 12.8 %all-to-all-start.1 = ((bf16[4,4,2,16,768]{4,3,2,1,0:T(8,128)(2,1)}), bf16[4,4,2,16,768]{4,3,2,1,0:T(8,128)(2,1)S(1)}, u32[]{:S(2)}, u32[]{:S(2)}) async-start(bf16[4,4,2,16,768]{4,3,2,1,0:T(8,128)(2,1)} %shard_map.65), calls=%async_computation.1 | async-start | bytes 1572864 | tf_op jit(solution)/shard_map/all_to_all | solution.py:50
  40.1 4.5 %collective-permute-start.3 = (bf16[768,128]{1,0:T(8,128)(2,1)S(1)}, bf16[768,128]{1,0:T(8,128)(2,1)S(1)}, u32[]{:S(2)}, u32[]{:S(2)}) collective-permute-start(bf16[768,128]{1,0:T(8,128)(2,1)S(1)} %bitcast.5), channel_id=1, source_target_pairs={{0,16},{1,17},{2,18},{3,19},{4,20},{5,21},{6,22},{7,23},{8,24},{9,... | collective-permute-start | bytes 589832 | tf_op jit(solution)/shard_map/ppermute | solution.py:35
  48.8 28.2 %copy-start.1 = (bf16[3,256,256]{2,1,0:T(8,128)(2,1)S(1)}, bf16[3,256,256]{2,1,0:T(8,128)(2,1)}, u32[]{:S(2)}) copy-start(bf16[3,256,256]{2,1,0:T(8,128)(2,1)} %lower.1) | copy-start | bytes 1179652
  48.8 25.2 %all-to-all-start.2 = ((bf16[4,4,4,16,768]{4,3,2,1,0:T(8,128)(2,1)}), bf16[4,4,4,16,768]{4,3,2,1,0:T(8,128)(2,1)S(1)}, u32[]{:S(2)}, u32[]{:S(2)}) async-start(bf16[4,4,4,16,768]{4,3,2,1,0:T(8,128)(2,1)} %shard_map.66), calls=%async_computation.2 | async-start | bytes 3145728 | tf_op jit(solution)/shard_map/all_to_all | solution.py:50
  54.2 8.6 %collective-permute-start.6 = (bf16[2,768,128]{2,1,0:T(8,128)(2,1)S(1)}, bf16[2,768,128]{2,1,0:T(8,128)(2,1)S(1)}, u32[]{:S(2)}, u32[]{:S(2)}) collective-permute-start(bf16[2,768,128]{2,1,0:T(8,128)(2,1)S(1)} %shard_map.67.own), channel_id=1, source_target_pairs={{0,64},{1,65},{2,66},{3,67},{4,68},{5,69},{6,70},{7,71},{8,72},{9,... | collective-permute-start | bytes 1179656 | tf_op jit(solution)/shard_map/ppermute | solution.py:35
  55.4 18.7 %collective-permute-start.5 = (bf16[2,768,128]{2,1,0:T(8,128)(2,1)S(1)}, bf16[2,768,128]{2,1,0:T(8,128)(2,1)S(1)}, u32[]{:S(2)}, u32[]{:S(2)}) collective-permute-start(bf16[2,768,128]{2,1,0:T(8,128)(2,1)S(1)} %shard_map.67.own), channel_id=1, source_target_pairs={{0,96},{1,97},{2,98},{3,99},{4,100},{5,101},{6,102},{7,103},{8,104... | collective-permute-start | bytes 1179656 | tf_op jit(solution)/shard_map/ppermute | solution.py:35
  55.7 18.4 %collective-permute-start.4 = (bf16[2,768,128]{2,1,0:T(8,128)(2,1)S(1)}, bf16[2,768,128]{2,1,0:T(8,128)(2,1)S(1)}, u32[]{:S(2)}, u32[]{:S(2)}) collective-permute-start(bf16[2,768,128]{2,1,0:T(8,128)(2,1)S(1)} %shard_map.67.own), channel_id=1, source_target_pairs={{0,32},{1,33},{2,34},{3,35},{4,36},{5,37},{6,38},{7,39},{8,40},{9,... | collective-permute-start | bytes 1179656 | tf_op jit(solution)/shard_map/ppermute | solution.py:35
  74.1 4.6 %copy-start.5 = (bf16[4,4,4,16,768]{4,3,2,1,0:T(8,128)(2,1)}, bf16[4,4,4,16,768]{4,3,2,1,0:T(8,128)(2,1)S(1)}, u32[]{:S(2)}) copy-start(bf16[4,4,4,16,768]{4,3,2,1,0:T(8,128)(2,1)S(1)} %all-to-all-done.2.refs_3_) | copy-start | bytes 4718596
  74.1 5.7 %collective-permute-start.7 = (bf16[4,4,4,16,768]{4,3,2,1,0:T(8,128)(2,1)S(1)}, bf16[4,4,4,16,768]{4,3,2,1,0:T(8,128)(2,1)}, u32[]{:S(2)}, u32[]{:S(2)}) collective-permute-start(bf16[4,4,4,16,768]{4,3,2,1,0:T(8,128)(2,1)S(1)} %all-to-all-done.2.refs_3_), channel_id=1, source_target_pairs={{0,1},{1,0},{2,3},{3,2},{4,5},{5,4},{6,7},{7,6},{8,9},{9,8},{10,11... | collective-permute-start | bytes 4718600 | tf_op jit(solution)/shard_map/ppermute | solution.py:35
  78.7 1.1 %copy-start = (bf16[768,1024]{1,0:T(8,128)(2,1)}, bf16[768,1024]{1,0:T(8,128)(2,1)S(1)}, u32[]{:S(2)}) copy-start(bf16[768,1024]{1,0:T(8,128)(2,1)S(1)} %shard_map.68.refs_2_) | copy-start | bytes 4718596
Sparse Core Ops, SparseCore 0:
  33.4 57.6 all-gather.2
